TPU v7x, 256 devices: a whole 4x4x8 slice. The times are simulated.
256 devices in a mesh: row: 32 (over y_hi, z, core), col: 8 (over x, y_lo).
Axes of the slice: x: 4, y: 4 (y_hi: 2, y_lo: 2; y = y_hi * 2 + y_lo), z: 8, core: 2. Of those that a mesh axis runs over, the one named last changes fastest.
Arguments:
- noise_latents: float32 [16384, 4096], P('row', 'col'), may hold values from -6 to 6
- data_latents: float32 [8192, 4096], P('col', 'row'), may hold values from -6 to 6
- flow_times: float32 [16384], P('row'), may hold values from 0 to 1
Outputs:
- velocity: float32 [16384, 4096], P('row', 'col')
- interpolant: float32 [16384, 4096], P('row', 'col')
All inputs are finite; a program needn't handle non-finite values.
Results may differ from a plain program's by a relative error of at most 0.0025.
Values may be sent and summed in bfloat16 or wider, within the bound.
A program may use at most 64 MiB of HBM per device.

v0:
```python
import math

import jax
import jax.numpy as jnp
from jax import lax
from jax.sharding import PartitionSpec as P

D = 4096
SWEEPS = 3


entropic_epsilon = 0.02


def row_logsumexp(scores):
    largest = lax.pmax(jnp.max(scores, axis=1), "col")
    sums = lax.psum(jnp.sum(jnp.exp(scores - largest[:, None]), axis=1), "col")
    return largest + jnp.log(sums)


def column_logsumexp(scores):
    largest = lax.pmax(jnp.max(scores, axis=0), "row")
    sums = lax.psum(jnp.sum(jnp.exp(scores - largest[None, :]), axis=0), "row")
    return largest + jnp.log(sums)


def local(noise_latents, data_latents, flow_times):
    noise_marginal_sum = noise_latents.shape[0] * lax.axis_size("row")
    data_marginal_sum = data_latents.shape[0] * lax.axis_size("col")
    noise_bf = lax.all_gather(noise_latents.astype(jnp.bfloat16), "col", axis=1, tiled=True)
    noise_wide = noise_bf.astype(jnp.float32)
    sq_noise = jnp.sum(noise_wide * noise_wide, axis=1)
    data_part = data_latents.astype(jnp.bfloat16)
    contract = (((1,), (1,)), ((), ()))
    data_bf = lax.all_gather(data_part, "row", axis=1, tiled=True)
    data_wide = data_bf.astype(jnp.float32)
    sq_data = jnp.sum(data_wide * data_wide, axis=1)
    inner = lax.dot_general(noise_bf, data_bf, contract, preferred_element_type=jnp.float32)
    squared_distance = (sq_noise[:, None] + sq_data[None, :] - 2.0 * inner) / D
    data_potential = jnp.zeros((data_part.shape[0],), jnp.float32)
    for sweep_index in range(SWEEPS):
        noise_potential = -entropic_epsilon * row_logsumexp(
            (data_potential[None, :] - squared_distance) / entropic_epsilon
        ) - entropic_epsilon * math.log(noise_marginal_sum)
        data_potential = -entropic_epsilon * column_logsumexp(
            (noise_potential[:, None] - squared_distance) / entropic_epsilon
        ) - entropic_epsilon * math.log(data_marginal_sum)
    noise_potential = -entropic_epsilon * row_logsumexp(
        (data_potential[None, :] - squared_distance) / entropic_epsilon
    ) - entropic_epsilon * math.log(noise_marginal_sum)
    transport_plan = jnp.exp(
        (noise_potential[:, None] + data_potential[None, :] - squared_distance) / entropic_epsilon
    ).astype(jnp.bfloat16)
    partial_sums = jnp.dot(transport_plan, data_bf, preferred_element_type=jnp.float32)
    width = noise_latents.shape[1]
    summed = lax.psum(partial_sums, "col")
    portion = lax.dynamic_slice_in_dim(summed, lax.axis_index("col") * width, width, 1)
    matched = noise_marginal_sum * portion
    velocity = matched - noise_latents
    interpolant = (1.0 - flow_times)[:, None] * noise_latents + flow_times[:, None] * matched
    return (velocity, interpolant)


def solution(mesh):
    in_specs = (P("row", "col"), P("col", "row"), P("row"))
    out_specs = (P("row", "col"), P("row", "col"))
    return jax.shard_map(local, mesh=mesh, in_specs=in_specs, out_specs=out_specs, check_vma=False)
```

profile of v0, /device:TPU:1, one launch (start us, length us, event | category | flops | bytes accessed | tf_op | source)
XLA Modules:
  0.0 1123.2 jit_solution(913827712814013932)
XLA Ops:
  7.2 0.0 copy-start.2
  7.2 0.0 all-gather.3.cloned.1.call-start
  7.2 2.1 convert_element_type.15
  9.4 0.0 all-gather.3.cloned.1.call-update
  9.4 0.0 all-gather.5.cloned.1.call-start
  9.4 0.0 copy-done.2
  9.4 0.7 convert_element_type.17
  10.2 0.0 all-gather.5.cloned.1.call-update
  10.2 0.0 all-reduce.2.cloned.1.call-start
  10.2 96.2 %all-gather.3.cloned.1.call-done = bf16[512,4096]{1,0:T(8,128)(2,1)} async-done(((bf16[512,512]{1,0:T(8,128)(2,1)}), bf16[512,4096]{1,0:T(8,128)(2,1)}) %all-gather.3.cloned.1.call-update) | async-done | bytes 4194320 | tf_op jit(solution)/shard_map/all_gather | solution.py:30
  106.5 3.1 multiply_reduce_fusion.1
  109.5 111.5 %all-gather.5.cloned.1.call-done = bf16[1024,4096]{1,0:T(8,128)(2,1)} async-done(((bf16[1024,128]{1,0:T(8,128)(2,1)}), bf16[1024,4096]{1,0:T(8,128)(2,1)}) %all-gather.5.cloned.1.call-update) | async-done | bytes 8388624 | tf_op jit(solution)/shard_map/all_gather | solution.py:35
  221.0 5.2 multiply_reduce_fusion
  226.2 0.5 copy-done
  226.8 6.8 fusion
  233.6 14.9 %pmax.49 = f32[512]{0:T(512)S(1)} all-reduce(f32[512]{0:T(512)S(1)} %get-tuple-element.6), channel_id=1, replica_groups=mesh['row'=32,'col'=8] {'col'}, use_global_device_ids=true, to_apply=%region_3.0 | all-reduce | flops 512 | bytes 4096 | tf_op jit(solution)/shard_map/pmax | solution.py:16
  248.5 0.6 exponential_reduce_fusion.6
  249.0 12.5 %psum.56 = f32[512]{0:T(512)S(1)} all-reduce(f32[512]{0:T(512)S(1)} %exponential_reduce_fusion.6), channel_id=1, replica_groups=mesh['row'=32,'col'=8] {'col'}, use_global_device_ids=true, to_apply=%region_5.0 | all-reduce | flops 512 | bytes 4096 | tf_op jit(solution)/shard_map/psum | solution.py:17
  261.5 0.3 fusion.1
  261.8 71.9 %pmax.50 = f32[1024]{0:T(1024)S(1)} all-reduce(f32[1024]{0:T(1024)S(1)} %fusion.1), channel_id=1, replica_groups=mesh['row'=32,'col'=8] {'row'}, use_global_device_ids=true, to_apply=%region_7.0 | all-reduce | flops 1024 | bytes 8192 | tf_op jit(solution)/shard_map/pmax | solution.py:22
  333.7 0.5 exponential_reduce_fusion.5
  334.2 65.0 %psum.57 = f32[1024]{0:T(1024)S(1)} all-reduce(f32[1024]{0:T(1024)S(1)} %exponential_reduce_fusion.5), channel_id=1, replica_groups=mesh['row'=32,'col'=8] {'row'}, use_global_device_ids=true, to_apply=%region_9.0 | all-reduce | flops 1024 | bytes 8192 | tf_op jit(solution)/shard_map/psum | solution.py:23
  399.2 0.3 fusion.2
  399.5 14.2 %pmax.51 = f32[512]{0:T(512)S(1)} all-reduce(f32[512]{0:T(512)S(1)} %fusion.2), channel_id=1, replica_groups=mesh['row'=32,'col'=8] {'col'}, use_global_device_ids=true, to_apply=%region_11.0 | all-reduce | flops 512 | bytes 4096 | tf_op jit(solution)/shard_map/pmax | solution.py:16
  413.7 0.6 exponential_reduce_fusion.4
  414.2 12.7 %psum.58 = f32[512]{0:T(512)S(1)} all-reduce(f32[512]{0:T(512)S(1)} %exponential_reduce_fusion.4), channel_id=1, replica_groups=mesh['row'=32,'col'=8] {'col'}, use_global_device_ids=true, to_apply=%region_13.0 | all-reduce | flops 512 | bytes 4096 | tf_op jit(solution)/shard_map/psum | solution.py:17
  426.9 0.3 fusion.3
  427.2 72.1 %pmax.52 = f32[1024]{0:T(1024)S(1)} all-reduce(f32[1024]{0:T(1024)S(1)} %fusion.3), channel_id=1, replica_groups=mesh['row'=32,'col'=8] {'row'}, use_global_device_ids=true, to_apply=%region_15.0 | all-reduce | flops 1024 | bytes 8192 | tf_op jit(solution)/shard_map/pmax | solution.py:22
  499.3 0.5 exponential_reduce_fusion.3
  499.8 65.0 %psum.59 = f32[1024]{0:T(1024)S(1)} all-reduce(f32[1024]{0:T(1024)S(1)} %exponential_reduce_fusion.3), channel_id=1, replica_groups=mesh['row'=32,'col'=8] {'row'}, use_global_device_ids=true, to_apply=%region_17.0 | all-reduce | flops 1024 | bytes 8192 | tf_op jit(solution)/shard_map/psum | solution.py:23
  564.8 0.3 fusion.4
  565.1 14.2 %pmax.53 = f32[512]{0:T(512)S(1)} all-reduce(f32[512]{0:T(512)S(1)} %fusion.4), channel_id=1, replica_groups=mesh['row'=32,'col'=8] {'col'}, use_global_device_ids=true, to_apply=%region_19.0 | all-reduce | flops 512 | bytes 4096 | tf_op jit(solution)/shard_map/pmax | solution.py:16
  579.3 0.6 exponential_reduce_fusion.2
  579.9 12.7 %psum.60 = f32[512]{0:T(512)S(1)} all-reduce(f32[512]{0:T(512)S(1)} %exponential_reduce_fusion.2), channel_id=1, replica_groups=mesh['row'=32,'col'=8] {'col'}, use_global_device_ids=true, to_apply=%region_21.0 | all-reduce | flops 512 | bytes 4096 | tf_op jit(solution)/shard_map/psum | solution.py:17
  592.6 0.3 fusion.5
  592.9 72.1 %pmax.54 = f32[1024]{0:T(1024)S(1)} all-reduce(f32[1024]{0:T(1024)S(1)} %fusion.5), channel_id=1, replica_groups=mesh['row'=32,'col'=8] {'row'}, use_global_device_ids=true, to_apply=%region_23.0 | all-reduce | flops 1024 | bytes 8192 | tf_op jit(solution)/shard_map/pmax | solution.py:22
  664.9 0.5 exponential_reduce_fusion.1
  665.4 65.0 %psum.61 = f32[1024]{0:T(1024)S(1)} all-reduce(f32[1024]{0:T(1024)S(1)} %exponential_reduce_fusion.1), channel_id=1, replica_groups=mesh['row'=32,'col'=8] {'row'}, use_global_device_ids=true, to_apply=%region_25.0 | all-reduce | flops 1024 | bytes 8192 | tf_op jit(solution)/shard_map/psum | solution.py:23
  730.5 0.3 fusion.6
  730.8 14.4 %pmax.55 = f32[512]{0:T(512)S(1)} all-reduce(f32[512]{0:T(512)S(1)} %fusion.6), channel_id=1, replica_groups=mesh['row'=32,'col'=8] {'col'}, use_global_device_ids=true, to_apply=%region_27.0 | all-reduce | flops 512 | bytes 4096 | tf_op jit(solution)/shard_map/pmax | solution.py:16
  745.1 0.6 exponential_reduce_fusion
  745.7 12.7 %psum.62 = f32[512]{0:T(512)S(1)} all-reduce(f32[512]{0:T(512)S(1)} %exponential_reduce_fusion), channel_id=1, replica_groups=mesh['row'=32,'col'=8] {'col'}, use_global_device_ids=true, to_apply=%region_29.0 | all-reduce | flops 512 | bytes 4096 | tf_op jit(solution)/shard_map/psum | solution.py:17
  758.4 10.4 fusion.7
  768.8 0.0 all-reduce.2.cloned.1.call-update
  768.8 0.6 copy-done.3
  769.4 344.5 %all-reduce.2.cloned.1.call-done = f32[512,4096]{1,0:T(8,128)} async-done(((f32[512,4096]{1,0:T(8,128)}), f32[512,4096]{1,0:T(8,128)}) %all-reduce.2.cloned.1.call-update) | async-done | bytes 8388624 | tf_op jit(solution)/shard_map/psum | solution.py:56
  1113.9 0.0 copy-done.1
  1113.9 2.8 multiply_add_fusion
  (11 shorter events, 0.1 us)
Async XLA Ops:
  7.2 2.3 copy-start.2
  7.2 99.3 %all-gather.3.cloned.1.call-start = ((), (), s32[]{:S(2)}) async-start(), calls=%async_computation | async-start | bytes 4718592 | tf_op jit(solution)/shard_map/all_gather | solution.py:30
  9.4 211.6 %all-gather.5.cloned.1.call-start = ((), (), s32[]{:S(2)}) async-start(), calls=%async_computation.1 | async-start | bytes 8650752 | tf_op jit(solution)/shard_map/all_gather | solution.py:35
  10.2 1103.7 %all-reduce.2.cloned.1.call-start = ((), (), s32[]{:S(2)}) async-start(), calls=%async_computation.2 | async-start | bytes 16777216 | tf_op jit(solution)/shard_map/psum | solution.py:56
  221.0 5.8 copy-start
  768.7 0.7 copy-start.3
  768.8 345.2 %copy-start.1 = (f32[512,512]{1,0:T(8,128)S(1)}, f32[512,512]{1,0:T(8,128)}, u32[]{:S(2)}) copy-start(f32[512,512]{1,0:T(8,128)} %param.3) | copy-start | bytes 3145732
Sparse Core Ops, SparseCore 0:
  10.4 96.0 all-gather.2
  109.6 111.3 all-gather.4
  768.9 344.9 all-reduce.1
where the time goes:
time: 1130 us; the launch traced here: 1120 us
  waiting for transfers between devices  552 us (49%)
  blocking collectives  519 us (46%)
  other arithmetic  19.5 us (2%)
  matrix products  17.1 us (2%)
  between operations  13.8 us (1%)
    psum x1, waiting for transfers between devices, local(): summed = lax.psum(partial_sums, 'col')  345 us
    pmax x3, blocking collectives, column_logsumexp(): largest = lax.pmax(jnp.max(scores, axis=0), 'row')  216 us
    psum x3, blocking collectives, column_logsumexp(): sums = lax.psum(jnp.sum(jnp.exp(scores - largest[None, :]), axis=0), 'row')  195 us
    all_gather x1, waiting for transfers between devices, local(): data_bf = lax.all_gather(data_part, 'row', axis=1, tiled=True)  111 us
    all_gather x1, waiting for transfers between devices, local(): lax.all_gather(noise_latents.astype(jnp.bfloat16), 'col', axis=1, tiled=T...  96.2 us
    pmax x4, blocking collectives, row_logsumexp(): largest = lax.pmax(jnp.max(scores, axis=1), 'col')  57.7 us
    psum x4, blocking collectives, row_logsumexp(): sums = lax.psum(jnp.sum(jnp.exp(scores - largest[:, None]), axis=1), 'col')  50.5 us
  transfers between devices with their start and end apart: 3, of which 3 were waited for; matrix products, arithmetic and copies ran while one was open for 0% of the time, Pallas kernels for 0%

commit v1 on v0

v1 whole, which is shorter than its diff:
```python
import math

import jax
import jax.numpy as jnp
from jax import lax
from jax.experimental import pallas as pl
from jax.experimental.pallas import tpu as pltpu
from jax.sharding import PartitionSpec as P

D = 4096
SWEEPS = 3
entropic_epsilon = 0.02
MESH = pl.DeviceIdType.MESH
LOG2E = 1.0 / math.log(2.0)

ROWS, COLS = 512, 1024
QS, QW = 16, 256
LANES = 128


def log2sumexp2(values):
    largest = jnp.max(values, axis=0, keepdims=True)
    sums = jnp.sum(jnp.exp2(values - largest), axis=0, keepdims=True)
    return largest + jnp.log(sums) * LOG2E


def kernel(noise_ref, data_ref, out_ref,
           nb, db, scores, plan, parts, got, lane_lse, noise_col, data_row, sq_n, sq_d,
           row_x, col_x, pair_x,
           n_send, n_recv, d_send, d_recv, s_send, s_recv,
           rx_send, rx_recv, cx_send, cx_recv, px_send, px_recv, m_send, m_recv):
    row, col = lax.axis_index("row"), lax.axis_index("col")
    yhi, z, core = row // 16, lax.rem(row // 2, 8), lax.rem(row, 2)
    x, ylo = col // 2, lax.rem(col, 2)
    chip = row // 2

    def at_x(shift, other=False):
        return lax.rem(x + shift + 4, 4) * 2 + (1 - ylo if other else ylo)

    def at_z(shift, other=False):
        return (1 - yhi if other else yhi) * 8 + lax.rem(z + shift + 8, 8)

    sibling = (row + 1 - 2 * core, col)

    barrier = pltpu.get_barrier_semaphore()
    pl.semaphore_signal(barrier, inc=1, device_id=sibling, device_id_type=MESH)

    def greet_col(k, _):
        pl.semaphore_signal(barrier, inc=1, device_id=(row, lax.rem(col + k, 8)), device_id_type=MESH)
        return 0

    def greet_row(k, _):
        pl.semaphore_signal(barrier, inc=1, device_id=(lax.rem(chip + k, 16) * 2 + core, col), device_id_type=MESH)
        return 0

    lax.fori_loop(1, 8, greet_col, 0)
    lax.fori_loop(1, 16, greet_row, 0)

    halfway = pl.ds(pl.multiple_of(core * LANES, LANES), LANES)
    db[chip, :, halfway] = data_ref[...].astype(jnp.bfloat16)
    for h in range(2):
        nb[2 * col + h] = noise_ref[:, h * QW:(h + 1) * QW].astype(jnp.bfloat16)
    pl.semaphore_wait(barrier, 23)

    sends = []

    def send_noise(chunk, to_col):
        copy = pltpu.make_async_remote_copy(
            nb.at[pl.ds(2 * chunk, 2)], nb.at[pl.ds(2 * chunk, 2)],
            n_send.at[len([s for s in sends if s[0] == "n"])], n_recv.at[chunk],
            device_id=(row, to_col), device_id_type=MESH)
        copy.start()
        sends.append(("n", copy))

    def wait_noise(chunk):
        pltpu.make_async_remote_copy(
            nb.at[pl.ds(2 * chunk, 2)], nb.at[pl.ds(2 * chunk, 2)], n_send.at[0], n_recv.at[chunk],
            device_id=(row, col), device_id_type=MESH).wait_recv()

    def send_data(q, to_chip):
        copy = pltpu.make_async_remote_copy(
            db.at[q, :, halfway], db.at[q, :, halfway],
            d_send.at[len([s for s in sends if s[0] == "d"])], d_recv.at[q],
            device_id=(to_chip * 2 + core, col), device_id_type=MESH)
        copy.start()
        sends.append(("d", copy))

    def send_sibling(q):
        copy = pltpu.make_async_remote_copy(
            db.at[q, :, halfway], db.at[q, :, halfway],
            s_send.at[len([s for s in sends if s[0] == "s"])], s_recv.at[q],
            device_id=sibling, device_id_type=MESH)
        copy.start()
        sends.append(("s", copy))

    def wait_data(q):
        pltpu.make_async_remote_copy(
            db.at[q, :, halfway], db.at[q, :, halfway], d_send.at[0], d_recv.at[q],
            device_id=sibling, device_id_type=MESH).wait_recv()

    otherway = pl.ds(pl.multiple_of((1 - core) * LANES, LANES), LANES)

    def wait_sibling(q):
        pltpu.make_async_remote_copy(
            db.at[q, :, otherway], db.at[q, :, otherway], s_send.at[0], s_recv.at[q],
            device_id=sibling, device_id_type=MESH).wait_recv()

    def pass_data(q, forward):
        wait_data(q)
        for shift in forward:
            send_data(q, at_z(shift))
        send_sibling(q)

    send_data(chip, at_z(0, True))
    send_data(chip, at_z(1))
    send_data(chip, at_z(-1))
    send_noise(col, at_x(0, True))
    send_noise(col, at_x(1))
    send_noise(col, at_x(-1))
    send_sibling(chip)

    pass_data(at_z(-1), (1,))
    pass_data(at_z(1), (-1,))
    pass_data(at_z(0, True), (1, -1))
    wait_noise(at_x(-1))
    send_noise(at_x(-1), at_x(1))
    wait_noise(at_x(1))
    wait_noise(at_x(0, True))
    send_noise(at_x(0, True), at_x(1))
    send_noise(at_x(0, True), at_x(-1))
    pass_data(at_z(-1, True), (1,))
    pass_data(at_z(1, True), (-1,))
    pass_data(at_z(-2), (1,))
    pass_data(at_z(2), (-1,))
    pass_data(at_z(-2, True), (1,))
    pass_data(at_z(2, True), (-1,))
    pass_data(at_z(-3), (1,))
    pass_data(at_z(3), ())
    wait_noise(at_x(1, True))
    send_noise(at_x(1, True), at_x(-1))
    wait_noise(at_x(-1, True))
    pass_data(at_z(-3, True), ())
    pass_data(at_z(3, True), (-1,))
    wait_noise(at_x(2))
    wait_noise(at_x(2, True))
    pass_data(at_z(4), ())
    pass_data(at_z(4, True), ())
    for q in range(QS):
        wait_sibling(q)

    scores[...] = jnp.zeros_like(scores)
    sq_n[...] = jnp.zeros_like(sq_n)
    sq_d[...] = jnp.zeros_like(sq_d)

    def block(q, _):
        def strip(t, _):
            at = pl.ds(pl.multiple_of(t * QW, QW), QW)
            scores[:, at] += lax.dot_general(
                nb[q], db[q, at, :], (((1,), (1,)), ((), ())), preferred_element_type=jnp.float32)
            wide = db[q, at, :].astype(jnp.float32)
            wide = wide * wide
            sq_d[at, :] += wide[:, :LANES] + wide[:, LANES:]
            return 0
        lax.fori_loop(0, COLS // QW, strip, 0)

        def norm(t, _):
            at = pl.ds(pl.multiple_of(t * LANES, LANES), LANES)
            wide = nb[q, at, :].astype(jnp.float32)
            wide = wide * wide
            sq_n[at, :] += wide[:, :LANES] + wide[:, LANES:]
            return 0
        lax.fori_loop(0, ROWS // LANES, norm, 0)
        return 0

    lax.fori_loop(0, QS, block, 0)

    scale = LOG2E / (entropic_epsilon * D)

    def norm_row(t, _):
        at = pl.ds(pl.multiple_of(t * LANES, LANES), LANES)
        data_row[:, at] = jnp.sum(sq_d[at, :].T, axis=0, keepdims=True)
        return 0

    lax.fori_loop(0, COLS // LANES, norm_row, 0)
    group = 32

    def score(t, _):
        at = pl.ds(pl.multiple_of(t * group, group), group)
        norms = jnp.sum(sq_n[at, :], axis=1, keepdims=True)
        scores[at, :] = (2.0 * scores[at, :] - norms - data_row[...]) * scale
        return 0

    lax.fori_loop(0, ROWS // group, score, 0)
    data_row[...] = jnp.zeros_like(data_row)

    def noise_step(e):
        def pass_over(t, _):
            at = pl.ds(pl.multiple_of(t * group, group), group)
            terms = [scores[at, c * LANES:(c + 1) * LANES] + data_row[:, c * LANES:(c + 1) * LANES]
                     for c in range(COLS // LANES)]
            largest = terms[0]
            for term in terms[1:]:
                largest = jnp.maximum(largest, term)
            sums = jnp.exp2(terms[0] - largest)
            for term in terms[1:]:
                sums = sums + jnp.exp2(term - largest)
            lane_lse[at, :] = largest + jnp.log(sums) * LOG2E
            return 0
        lax.fori_loop(0, ROWS // group, pass_over, 0)
        for b in range(ROWS // LANES):
            at = slice(b * LANES, (b + 1) * LANES)
            row_x[e, pl.ds(col, 1), :, at] = log2sumexp2(lane_lse[at, :].T)[None]

        def send(k, _):
            pltpu.make_async_remote_copy(
                row_x.at[e, col], row_x.at[e, col], rx_send.at[e, k], rx_recv.at[e, col],
                device_id=(row, lax.rem(col + k, 8)), device_id_type=MESH).start()
            return 0

        def arrive(k, _):
            source = lax.rem(col + k, 8)
            pltpu.make_async_remote_copy(
                row_x.at[e, source], row_x.at[e, source], rx_send.at[e, k], rx_recv.at[e, source],
                device_id=(row, source), device_id_type=MESH).wait()
            return 0

        lax.fori_loop(1, 8, send, 0)
        lax.fori_loop(1, 8, arrive, 0)
        potential = -log2sumexp2(row_x[e])[0] - math.log2(16384)
        for b in range(ROWS // LANES):
            at = slice(b * LANES, (b + 1) * LANES)
            noise_col[at, :] = jnp.broadcast_to(potential[:, at], (LANES, LANES)).T

    def data_step(e):
        def pass_over(t, _):
            at = pl.ds(pl.multiple_of(t * LANES, LANES), LANES)
            partial = []
            for h in range(2):
                rows = slice(h * 256, (h + 1) * 256)
                terms = (scores[rows, at] + noise_col[rows, :]).reshape(32, 8, LANES)
                partial.append(log2sumexp2(terms)[0])
            pair_x[e, 0, :, at] = log2sumexp2(jnp.concatenate(partial, axis=0))
            return 0
        lax.fori_loop(0, COLS // LANES, pass_over, 0)
        swap = pltpu.make_async_remote_copy(
            pair_x.at[e, 0], pair_x.at[e, 1], px_send.at[e], px_recv.at[e],
            device_id=sibling, device_id_type=MESH)
        swap.start()
        swap.wait()
        col_x[e, pl.ds(chip, 1)] = log2sumexp2(pair_x[e])

        def send(k, _):
            pltpu.make_async_remote_copy(
                col_x.at[e, chip], col_x.at[e, chip], cx_send.at[e, k], cx_recv.at[e, chip],
                device_id=(lax.rem(chip + k, 16) * 2 + core, col), device_id_type=MESH).start()
            return 0

        def arrive(k, _):
            source = lax.rem(chip + k, 16)
            pltpu.make_async_remote_copy(
                col_x.at[e, source], col_x.at[e, source], cx_send.at[e, k], cx_recv.at[e, source],
                device_id=(source * 2 + core, col), device_id_type=MESH).wait()
            return 0

        lax.fori_loop(1, 16, send, 0)
        lax.fori_loop(1, 16, arrive, 0)
        data_row[...] = -log2sumexp2(col_x[e])[0] - math.log2(8192)

    for e in range(SWEEPS):
        noise_step(e)
        data_step(e)
    noise_step(SWEEPS)

    def transport(t, _):
        at = pl.ds(pl.multiple_of(t * group, group), group)
        for c in range(COLS // LANES):
            lanes = slice(c * LANES, (c + 1) * LANES)
            plan[at, lanes] = jnp.exp2(noise_col[at, :] + data_row[:, lanes] + scores[at, lanes]).astype(jnp.bfloat16)
        return 0

    lax.fori_loop(0, ROWS // group, transport, 0)

    def spread(k, _):
        target = lax.rem(col + k, 8)
        for h in range(2):
            parts[k, h] = (16384.0 * jnp.dot(
                plan[...], db[2 * target + h], preferred_element_type=jnp.float32)).astype(jnp.bfloat16)
        pltpu.make_async_remote_copy(
            parts.at[k], got.at[k], m_send.at[k], m_recv.at[k],
            device_id=(row, target), device_id_type=MESH).start()
        return 0

    lax.fori_loop(1, 8, spread, 0)
    for h in range(2):
        out_ref[:, h * QW:(h + 1) * QW] = 16384.0 * jnp.dot(
            plan[...], db[2 * col + h], preferred_element_type=jnp.float32)

    def collect(k, _):
        pltpu.make_async_remote_copy(
            parts.at[k], got.at[k], m_send.at[k], m_recv.at[k],
            device_id=(row, lax.rem(col + k, 8)), device_id_type=MESH).wait()
        return 0

    lax.fori_loop(1, 8, collect, 0)

    def total(t, _):
        at = pl.ds(pl.multiple_of(t * group, group), group)
        for h in range(2):
            lanes = slice(h * QW, (h + 1) * QW)
            value = out_ref[at, lanes]
            for k in range(1, 8):
                value = value + got[k, h, at, :].astype(jnp.float32)
            out_ref[at, lanes] = value
        return 0

    lax.fori_loop(0, ROWS // group, total, 0)
    for _, copy in sends:
        copy.wait_send()


def local(noise_latents, data_latents, flow_times):
    bf16, f32 = jnp.bfloat16, jnp.float32
    vmem, dma = pltpu.VMEM, pltpu.SemaphoreType.DMA
    matched = pl.pallas_call(
        kernel,
        out_shape=jax.ShapeDtypeStruct((ROWS, 2 * QW), f32),
        in_specs=[pl.BlockSpec(memory_space=pltpu.VMEM)] * 2,
        out_specs=pl.BlockSpec(memory_space=pltpu.VMEM),
        scratch_shapes=[
            vmem((QS, ROWS, QW), bf16), vmem((QS, COLS, QW), bf16), vmem((ROWS, COLS), f32), vmem((ROWS, COLS), bf16),
            vmem((8, 2, ROWS, QW), bf16), vmem((8, 2, ROWS, QW), bf16),
            vmem((ROWS, LANES), f32), vmem((ROWS, LANES), f32), vmem((1, COLS), f32),
            vmem((ROWS, LANES), f32), vmem((COLS, LANES), f32),
            vmem((SWEEPS + 1, 8, 1, ROWS), f32), vmem((SWEEPS, QS, 1, COLS), f32), vmem((SWEEPS, 2, 1, COLS), f32),
            dma((8,)), dma((8,)), dma((16,)), dma((16,)), dma((16,)), dma((16,)),
            dma((SWEEPS + 1, 8)), dma((SWEEPS + 1, 8)), dma((SWEEPS, 16)), dma((SWEEPS, 16)),
            dma((SWEEPS,)), dma((SWEEPS,)), dma((8,)), dma((8,)),
        ],
        compiler_params=pltpu.CompilerParams(
            collective_id=0, has_side_effects=True, vmem_limit_bytes=48 << 20),
        name="sinkhorn",
    )(noise_latents, data_latents)
    velocity = matched - noise_latents
    interpolant = (1.0 - flow_times)[:, None] * noise_latents + flow_times[:, None] * matched
    return (velocity, interpolant)


def solution(mesh):
    in_specs = (P("row", "col"), P("col", "row"), P("row"))
    out_specs = (P("row", "col"), P("row", "col"))
    return jax.shard_map(local, mesh=mesh, in_specs=in_specs, out_specs=out_specs, check_vma=False)
```

time: 1130 us -> 198 us (0.18)
  the two profiles are of different devices: /device:TPU:1 before, /device:TPU:28 now
where the time goes in v1:
time: 198 us
  Pallas kernels  193 us (97%)
  local copies, waits for them, and re-layouts  2.27 us (1%)
  other arithmetic  2.18 us (1%)
    pallas_call x1, Pallas kernels, local(): pl.pallas_call(kernel, out_shape=jax.ShapeDtypeStruct((ROWS, 2 * QW), f32...  193 us

profile of v1, /device:TPU:28, one launch (start us, length us, event | category | flops | bytes accessed | tf_op | source)
XLA Modules:
  0.0 198.1 jit_solution(9590095621650693844)
XLA Ops:
  0.6 0.7 broadcast_subtract_fusion
  1.3 0.0 copy-start
  1.3 1.2 copy-done
  2.5 0.0 copy-start.1
  2.5 1.0 copy-done.1
  3.6 0.0 copy-start.2
  3.6 193.0 %sinkhorn.1 = f32[512,512]{1,0:T(8,128)S(1)} custom-call(f32[512,512]{1,0:T(8,128)S(1)} %copy-done, f32[1024,128]{1,0:T(8,128)S(1)} %copy-done.1), custom_call_target="tpu_custom_call" | custom-call | tf_op jit(solution)/shard_map/sinkhorn/pallas_call | solution.py:324
  196.6 0.0 copy-done.2
  196.6 1.5 multiply_add_fusion
Async XLA Ops:
  1.3 1.2 copy-start
  2.5 1.0 copy-start.1
  3.6 193.0 %copy-start.2 = (f32[512]{0:T(512)S(1)}, f32[512]{0:T(512)}, u32[]{:S(2)}) copy-start(f32[512]{0:T(512)} %param.5) | copy-start | bytes 6148

commit v2 on v1

--- a/solution.py
+++ b/solution.py
@@ -16,6 +16,8 @@
 ROWS, COLS = 512, 1024
 QS, QW = 16, 256
 LANES = 128
+X_FIRST = 288
+Y_FIRST = ROWS - X_FIRST
 
 
 def log2sumexp2(values):
@@ -24,8 +26,9 @@
     return largest + jnp.log(sums) * LOG2E
 
 
-def kernel(noise_ref, data_ref, out_ref,
-           nb, db, scores, plan, parts, got, lane_lse, noise_col, data_row, sq_n, sq_d,
+def kernel(noise_hbm, data_hbm, out_ref,
+           noise_ref, data_ref, load_sem,
+           nb, db, scores, plan, x_parts, x_got, y_parts, y_got, y_sum, lane_lse, noise_col, weight_col, data_row, sq_n, sq_d,
            row_x, col_x, pair_x,
            n_send, n_recv, d_send, d_recv, s_send, s_recv,
            rx_send, rx_recv, cx_send, cx_recv, px_send, px_recv, m_send, m_recv):
@@ -40,7 +43,18 @@
     def at_z(shift, other=False):
         return (1 - yhi if other else yhi) * 8 + lax.rem(z + shift + 8, 8)
 
+    def away(k):
+        return lax.rem(4 + jnp.where(lax.rem(k, 2) == 1, (k + 1) // 2, -(k // 2)), 8)
+
+    def row_peer(k):
+        other = jnp.where(k < 8, 1 - yhi, yhi)
+        return other * 8 + lax.rem(z + away(lax.rem(k, 8)), 8)
+
     sibling = (row + 1 - 2 * core, col)
+    load_noise = pltpu.make_async_copy(noise_hbm, noise_ref, load_sem.at[0])
+    load_data = pltpu.make_async_copy(data_hbm, data_ref, load_sem.at[1])
+    load_data.start()
+    load_noise.start()
 
     barrier = pltpu.get_barrier_semaphore()
     pl.semaphore_signal(barrier, inc=1, device_id=sibling, device_id_type=MESH)
@@ -50,16 +64,21 @@
         return 0
 
     def greet_row(k, _):
-        pl.semaphore_signal(barrier, inc=1, device_id=(lax.rem(chip + k, 16) * 2 + core, col), device_id_type=MESH)
+        pl.semaphore_signal(barrier, inc=1, device_id=(row_peer(k) * 2 + core, col), device_id_type=MESH)
         return 0
 
+    lax.fori_loop(0, 15, greet_row, 0)
     lax.fori_loop(1, 8, greet_col, 0)
-    lax.fori_loop(1, 16, greet_row, 0)
 
     halfway = pl.ds(pl.multiple_of(core * LANES, LANES), LANES)
+    load_data.wait()
     db[chip, :, halfway] = data_ref[...].astype(jnp.bfloat16)
+    load_noise.wait()
     for h in range(2):
         nb[2 * col + h] = noise_ref[:, h * QW:(h + 1) * QW].astype(jnp.bfloat16)
+    scores[...] = jnp.zeros_like(scores)
+    sq_n[...] = jnp.zeros_like(sq_n)
+    sq_d[...] = jnp.zeros_like(sq_d)
     pl.semaphore_wait(barrier, 23)
 
     sends = []
@@ -110,6 +129,49 @@
         for shift in forward:
             send_data(q, at_z(shift))
         send_sibling(q)
+
+    def level(c):
+        ahead = lax.rem(2 * lax.rem(c, 4) - z + 8, 8)
+        after = lax.rem(ahead + 1, 8)
+        far = jnp.maximum(jnp.minimum(ahead, 8 - ahead), jnp.minimum(after, 8 - after))
+        shift = lax.rem(c // 2 - x + 4, 4)
+        late = jnp.logical_and(lax.rem(shift, 2) == 1, lax.rem(c, 2) != ylo)
+        return jnp.where(far == 4, 4, jnp.where(shift == 2, 3, jnp.where(jnp.logical_or(far == 3, late), 2, 1)))
+
+    def multiply(now):
+        def chunk(c, _):
+            @pl.when(level(c) == now)
+            def _():
+                total = scores[...]
+                for h in range(2):
+                    total += lax.dot_general(
+                        nb[2 * c + h], db[2 * c + h], (((1,), (1,)), ((), ())), preferred_element_type=jnp.float32)
+                scores[...] = total
+
+                def data_norm(t, _):
+                    at = pl.ds(pl.multiple_of(t * LANES, LANES), LANES)
+                    squares = sq_d[at, :]
+                    for h in range(2):
+                        wide = db[2 * c + h, at, :].astype(jnp.float32)
+                        wide = wide * wide
+                        squares = squares + (wide[:, :LANES] + wide[:, LANES:])
+                    sq_d[at, :] = squares
+                    return 0
+
+                def noise_norm(t, _):
+                    at = pl.ds(pl.multiple_of(t * LANES, LANES), LANES)
+                    squares = sq_n[at, :]
+                    for h in range(2):
+                        wide = nb[2 * c + h, at, :].astype(jnp.float32)
+                        wide = wide * wide
+                        squares = squares + (wide[:, :LANES] + wide[:, LANES:])
+                    sq_n[at, :] = squares
+                    return 0
+
+                lax.fori_loop(0, COLS // LANES, data_norm, 0)
+                lax.fori_loop(0, ROWS // LANES, noise_norm, 0)
+            return 0
+        lax.fori_loop(0, 8, chunk, 0)
 
     send_data(chip, at_z(0, True))
     send_data(chip, at_z(1))
@@ -134,6 +196,10 @@
     pass_data(at_z(2), (-1,))
     pass_data(at_z(-2, True), (1,))
     pass_data(at_z(2, True), (-1,))
+    for shift in (0, 1, -1, 2, -2):
+        wait_sibling(at_z(shift))
+        wait_sibling(at_z(shift, True))
+    multiply(1)
     pass_data(at_z(-3), (1,))
     pass_data(at_z(3), ())
     wait_noise(at_x(1, True))
@@ -141,38 +207,18 @@
     wait_noise(at_x(-1, True))
     pass_data(at_z(-3, True), ())
     pass_data(at_z(3, True), (-1,))
+    for shift in (3, -3):
+        wait_sibling(at_z(shift))
+        wait_sibling(at_z(shift, True))
+    multiply(2)
     wait_noise(at_x(2))
     wait_noise(at_x(2, True))
+    multiply(3)
     pass_data(at_z(4), ())
     pass_data(at_z(4, True), ())
-    for q in range(QS):
-        wait_sibling(q)
-
-    scores[...] = jnp.zeros_like(scores)
-    sq_n[...] = jnp.zeros_like(sq_n)
-    sq_d[...] = jnp.zeros_like(sq_d)
-
-    def block(q, _):
-        def strip(t, _):
-            at = pl.ds(pl.multiple_of(t * QW, QW), QW)
-            scores[:, at] += lax.dot_general(
-                nb[q], db[q, at, :], (((1,), (1,)), ((), ())), preferred_element_type=jnp.float32)
-            wide = db[q, at, :].astype(jnp.float32)
-            wide = wide * wide
-            sq_d[at, :] += wide[:, :LANES] + wide[:, LANES:]
-            return 0
-        lax.fori_loop(0, COLS // QW, strip, 0)
-
-        def norm(t, _):
-            at = pl.ds(pl.multiple_of(t * LANES, LANES), LANES)
-            wide = nb[q, at, :].astype(jnp.float32)
-            wide = wide * wide
-            sq_n[at, :] += wide[:, :LANES] + wide[:, LANES:]
-            return 0
-        lax.fori_loop(0, ROWS // LANES, norm, 0)
-        return 0
-
-    lax.fori_loop(0, QS, block, 0)
+    wait_sibling(at_z(4))
+    wait_sibling(at_z(4, True))
+    multiply(4)
 
     scale = LOG2E / (entropic_epsilon * D)
 
@@ -184,20 +230,24 @@
     lax.fori_loop(0, COLS // LANES, norm_row, 0)
     group = 32
 
-    def score(t, _):
-        at = pl.ds(pl.multiple_of(t * group, group), group)
-        norms = jnp.sum(sq_n[at, :], axis=1, keepdims=True)
-        scores[at, :] = (2.0 * scores[at, :] - norms - data_row[...]) * scale
-        return 0
-
-    lax.fori_loop(0, ROWS // group, score, 0)
-    data_row[...] = jnp.zeros_like(data_row)
+    def to_column(column_ref, line):
+        for b in range(ROWS // LANES):
+            at = slice(b * LANES, (b + 1) * LANES)
+            column_ref[at, :] = jnp.broadcast_to(line[:, at], (LANES, LANES)).T
 
     def noise_step(e):
         def pass_over(t, _):
             at = pl.ds(pl.multiple_of(t * group, group), group)
-            terms = [scores[at, c * LANES:(c + 1) * LANES] + data_row[:, c * LANES:(c + 1) * LANES]
-                     for c in range(COLS // LANES)]
+            if e == 0:
+                norms = jnp.sum(sq_n[at, :], axis=1, keepdims=True)
+                terms = []
+                for c in range(COLS // LANES):
+                    lanes = slice(c * LANES, (c + 1) * LANES)
+                    terms.append((2.0 * scores[at, lanes] - norms - data_row[:, lanes]) * scale)
+                    scores[at, lanes] = terms[c]
+            else:
+                terms = [scores[at, c * LANES:(c + 1) * LANES] + data_row[:, c * LANES:(c + 1) * LANES]
+                         for c in range(COLS // LANES)]
             largest = terms[0]
             for term in terms[1:]:
                 largest = jnp.maximum(largest, term)
@@ -225,11 +275,7 @@
             return 0
 
         lax.fori_loop(1, 8, send, 0)
-        lax.fori_loop(1, 8, arrive, 0)
-        potential = -log2sumexp2(row_x[e])[0] - math.log2(16384)
-        for b in range(ROWS // LANES):
-            at = slice(b * LANES, (b + 1) * LANES)
-            noise_col[at, :] = jnp.broadcast_to(potential[:, at], (LANES, LANES)).T
+        return lambda: lax.fori_loop(1, 8, arrive, 0)
 
     def data_step(e):
         def pass_over(t, _):
@@ -252,68 +298,169 @@
         def send(k, _):
             pltpu.make_async_remote_copy(
                 col_x.at[e, chip], col_x.at[e, chip], cx_send.at[e, k], cx_recv.at[e, chip],
-                device_id=(lax.rem(chip + k, 16) * 2 + core, col), device_id_type=MESH).start()
+                device_id=(row_peer(k) * 2 + core, col), device_id_type=MESH).start()
             return 0
 
         def arrive(k, _):
-            source = lax.rem(chip + k, 16)
+            source = row_peer(k)
             pltpu.make_async_remote_copy(
                 col_x.at[e, source], col_x.at[e, source], cx_send.at[e, k], cx_recv.at[e, source],
                 device_id=(source * 2 + core, col), device_id_type=MESH).wait()
             return 0
 
-        lax.fori_loop(1, 16, send, 0)
-        lax.fori_loop(1, 16, arrive, 0)
+        lax.fori_loop(0, 15, send, 0)
+        lax.fori_loop(0, 15, arrive, 0)
         data_row[...] = -log2sumexp2(col_x[e])[0] - math.log2(8192)
 
     for e in range(SWEEPS):
-        noise_step(e)
+        noise_step(e)()
+        to_column(noise_col, -log2sumexp2(row_x[e])[0] - math.log2(16384))
         data_step(e)
-    noise_step(SWEEPS)
+
+    last_arrives = noise_step(SWEEPS)
+    to_column(noise_col, row_x[SWEEPS, col])
 
     def transport(t, _):
         at = pl.ds(pl.multiple_of(t * group, group), group)
         for c in range(COLS // LANES):
             lanes = slice(c * LANES, (c + 1) * LANES)
-            plan[at, lanes] = jnp.exp2(noise_col[at, :] + data_row[:, lanes] + scores[at, lanes]).astype(jnp.bfloat16)
+            plan[at, lanes] = jnp.exp2(data_row[:, lanes] + scores[at, lanes] - noise_col[at, :]).astype(jnp.bfloat16)
         return 0
 
     lax.fori_loop(0, ROWS // group, transport, 0)
 
-    def spread(k, _):
-        target = lax.rem(col + k, 8)
-        for h in range(2):
-            parts[k, h] = (16384.0 * jnp.dot(
-                plan[...], db[2 * target + h], preferred_element_type=jnp.float32)).astype(jnp.bfloat16)
-        pltpu.make_async_remote_copy(
-            parts.at[k], got.at[k], m_send.at[k], m_recv.at[k],
-            device_id=(row, target), device_id_type=MESH).start()
-        return 0
-
-    lax.fori_loop(1, 8, spread, 0)
+    top, low = slice(0, X_FIRST), slice(X_FIRST, ROWS)
+    half = Y_FIRST // 2
+    SELF, LEFT, RIGHT, MATE = range(4)
+
+    def chunk_sum(rows, target, h):
+        return jnp.dot(plan[rows, :], db[2 * target + h], preferred_element_type=jnp.float32)
+
+    def weigh(value, who, rows):
+        weight = weight_col[who, rows, :]
+        return jnp.concatenate([value[:, :LANES] * weight, value[:, LANES:] * weight], axis=1)
+
+    def for_halves(body):
+        def step(h, _):
+            body(h)
+            return 0
+        lax.fori_loop(0, 2, step, 0)
+
+    def fill(ref, slot, rows, target, add=(), weighed=True):
+        def one(h):
+            value = chunk_sum(rows, target, h)
+            if weighed:
+                value = weigh(value, SELF, rows)
+            for other, other_slot, who in add:
+                term = other[other_slot, h].astype(jnp.float32)
+                value = value + (term if who is None else weigh(term, who, rows))
+            ref[slot, h] = value.astype(jnp.bfloat16)
+        for_halves(one)
+
+    def x_copy(slot, to_col):
+        return pltpu.make_async_remote_copy(
+            x_parts.at[slot], x_got.at[slot], m_send.at[slot], m_recv.at[slot],
+            device_id=(row, to_col), device_id_type=MESH)
+
+    def y_copy(slot, to_col):
+        return pltpu.make_async_remote_copy(
+            y_parts.at[slot], y_got.at[slot], m_send.at[7 + slot], m_recv.at[7 + slot],
+            device_id=(row, to_col), device_id_type=MESH)
+
+    def y_half(which, to_col):
+        at = pl.ds(which * half, half)
+        return pltpu.make_async_remote_copy(
+            y_parts.at[4, :, at, :], y_got.at[4, :, at, :], m_send.at[14 + which], m_recv.at[14 + which],
+            device_id=(row, to_col), device_id_type=MESH)
+
+    right, left = at_x(1), at_x(-1)
+    mate_col = at_x(0, True)
+    x_copies = [x_copy(slot, to) for slot, to in enumerate((right, left, right, left, right, left, mate_col))]
+    y_copies = {slot: y_copy(slot, to) for slot, to in ((0, mate_col), (1, mate_col), (2, mate_col), (3, mate_col), (5, right), (6, left))}
+    y_halves = [y_half(0, right), y_half(1, left)]
+
+    fill(x_parts, 0, top, at_x(2), weighed=False)
+    x_copies[0].start()
+    fill(x_parts, 1, top, at_x(2, True), weighed=False)
+    x_copies[1].start()
+    for slot, target in enumerate((at_x(2, True), at_x(1, True), at_x(-1, True), mate_col)):
+        fill(y_parts, slot, low, target, weighed=False)
+        y_copies[slot].start()
+
+    last_arrives()
+    whole = log2sumexp2(row_x[SWEEPS])[0]
+    for who, source in enumerate((col, left, right, mate_col)):
+        to_column(weight_col.at[who], jnp.exp2(row_x[SWEEPS, source] - whole))
+
+    fill(x_parts, 2, top, at_x(1, True))
+    x_copies[2].start()
+    y_copies[0].wait_recv()
+    fill(y_parts, 4, low, at_x(2), add=[(y_got, 0, MATE)])
+    y_halves[0].start()
+    y_halves[1].start()
+    x_copies[0].wait_recv()
+    fill(x_parts, 4, top, right, add=[(x_got, 0, LEFT)])
+    x_copies[4].start()
+    x_copies[1].wait_recv()
+    fill(x_parts, 5, top, at_x(-1, True), add=[(x_got, 1, RIGHT)])
+    x_copies[5].start()
+    fill(x_parts, 3, top, left)
+    x_copies[3].start()
+
+    def add_half(slot, which):
+        at = pl.ds(which * half, half)
+
+        def one(h):
+            y_parts[slot, h, at, :] = (
+                y_sum[h, at, :] + y_got[4, h, at, :].astype(jnp.float32)).astype(jnp.bfloat16)
+            rest = pl.ds((1 - which) * half, half)
+            y_parts[slot, h, rest, :] = y_sum[h, rest, :].astype(jnp.bfloat16)
+        for_halves(one)
+
+    def fill_sum(target, got_slot):
+        def one(h):
+            y_sum[h] = (weigh(chunk_sum(low, target, h), SELF, low)
+                        + weigh(y_got[got_slot, h].astype(jnp.float32), MATE, low))
+        for_halves(one)
+
+    y_copies[1].wait_recv()
+    fill_sum(right, 1)
+    y_halves[0].wait_recv()
+    add_half(5, 0)
+    y_copies[5].start()
+    y_copies[2].wait_recv()
+    fill_sum(left, 2)
+    y_halves[1].wait_recv()
+    add_half(6, 1)
+    y_copies[6].start()
+
+    x_copies[2].wait_recv()
+    x_copies[5].wait_recv()
+    fill(x_parts, 6, top, mate_col, add=[(x_got, 2, None), (x_got, 5, None)])
+    x_copies[6].start()
+
+    y_copies[3].wait_recv()
+    fill_sum(col, 3)
     for h in range(2):
-        out_ref[:, h * QW:(h + 1) * QW] = 16384.0 * jnp.dot(
-            plan[...], db[2 * col + h], preferred_element_type=jnp.float32)
-
-    def collect(k, _):
-        pltpu.make_async_remote_copy(
-            parts.at[k], got.at[k], m_send.at[k], m_recv.at[k],
-            device_id=(row, lax.rem(col + k, 8)), device_id_type=MESH).wait()
-        return 0
-
-    lax.fori_loop(1, 8, collect, 0)
-
-    def total(t, _):
-        at = pl.ds(pl.multiple_of(t * group, group), group)
-        for h in range(2):
-            lanes = slice(h * QW, (h + 1) * QW)
-            value = out_ref[at, lanes]
-            for k in range(1, 8):
-                value = value + got[k, h, at, :].astype(jnp.float32)
-            out_ref[at, lanes] = value
-        return 0
-
-    lax.fori_loop(0, ROWS // group, total, 0)
+        lanes = slice(h * QW, (h + 1) * QW)
+        out_ref[top, lanes] = weigh(chunk_sum(top, col, h), SELF, top)
+    x_copies[3].wait_recv()
+    x_copies[4].wait_recv()
+    for h in range(2):
+        lanes = slice(h * QW, (h + 1) * QW)
+        out_ref[top, lanes] += x_got[3, h].astype(jnp.float32) + x_got[4, h].astype(jnp.float32)
+    y_copies[5].wait_recv()
+    y_copies[6].wait_recv()
+    for h in range(2):
+        lanes = slice(h * QW, (h + 1) * QW)
+        out_ref[low, lanes] = y_sum[h] + (y_got[5, h].astype(jnp.float32) + y_got[6, h].astype(jnp.float32))
+    x_copies[6].wait_recv()
+    for h in range(2):
+        lanes = slice(h * QW, (h + 1) * QW)
+        out_ref[top, lanes] += x_got[6, h].astype(jnp.float32)
+
+    for copy in x_copies + list(y_copies.values()) + y_halves:
+        copy.wait_send()
     for _, copy in sends:
         copy.wait_send()
 
@@ -324,17 +471,19 @@
     matched = pl.pallas_call(
         kernel,
         out_shape=jax.ShapeDtypeStruct((ROWS, 2 * QW), f32),
-        in_specs=[pl.BlockSpec(memory_space=pltpu.VMEM)] * 2,
+        in_specs=[pl.BlockSpec(memory_space=pl.ANY)] * 2,
         out_specs=pl.BlockSpec(memory_space=pltpu.VMEM),
         scratch_shapes=[
+            vmem((ROWS, 2 * QW), f32), vmem((COLS, LANES), f32), dma((2,)),
             vmem((QS, ROWS, QW), bf16), vmem((QS, COLS, QW), bf16), vmem((ROWS, COLS), f32), vmem((ROWS, COLS), bf16),
-            vmem((8, 2, ROWS, QW), bf16), vmem((8, 2, ROWS, QW), bf16),
-            vmem((ROWS, LANES), f32), vmem((ROWS, LANES), f32), vmem((1, COLS), f32),
+            vmem((7, 2, X_FIRST, QW), bf16), vmem((7, 2, X_FIRST, QW), bf16),
+            vmem((7, 2, Y_FIRST, QW), bf16), vmem((7, 2, Y_FIRST, QW), bf16), vmem((2, Y_FIRST, QW), f32),
+            vmem((ROWS, LANES), f32), vmem((ROWS, LANES), f32), vmem((4, ROWS, LANES), f32), vmem((1, COLS), f32),
             vmem((ROWS, LANES), f32), vmem((COLS, LANES), f32),
             vmem((SWEEPS + 1, 8, 1, ROWS), f32), vmem((SWEEPS, QS, 1, COLS), f32), vmem((SWEEPS, 2, 1, COLS), f32),
             dma((8,)), dma((8,)), dma((16,)), dma((16,)), dma((16,)), dma((16,)),
             dma((SWEEPS + 1, 8)), dma((SWEEPS + 1, 8)), dma((SWEEPS, 16)), dma((SWEEPS, 16)),
-            dma((SWEEPS,)), dma((SWEEPS,)), dma((8,)), dma((8,)),
+            dma((SWEEPS,)), dma((SWEEPS,)), dma((16,)), dma((16,)),
         ],
         compiler_params=pltpu.CompilerParams(
             collective_id=0, has_side_effects=True, vmem_limit_bytes=48 << 20),

time: 198 us -> 144 us (0.73)
  the two profiles are of different devices: /device:TPU:28 before, /device:TPU:1 now
where the time goes in v2:
time: 144 us; the launch traced here: 143 us
  Pallas kernels  138 us (96%)
  local copies, waits for them, and re-layouts  2.27 us (2%)
  other arithmetic  2.18 us (2%)
    pallas_call x1, Pallas kernels, local(): pl.pallas_call(kernel, out_shape=jax.ShapeDtypeStruct((ROWS, 2 * QW), f32...  138 us

profile of v2, /device:TPU:1, one launch (start us, length us, event | category | flops | bytes accessed | tf_op | source)
XLA Modules:
  0.0 143.0 jit_solution(14895598946015837097)
XLA Ops:
  0.6 0.7 broadcast_subtract_fusion
  1.3 0.0 copy-start
  1.3 1.2 copy-done
  2.5 0.0 copy-start.1
  2.5 1.0 copy-done.1
  3.6 0.0 copy-start.2
  3.6 137.9 %sinkhorn.1 = f32[512,512]{1,0:T(8,128)S(1)} custom-call(f32[512,512]{1,0:T(8,128)S(1)} %copy-done, f32[1024,128]{1,0:T(8,128)S(1)} %copy-done.1), custom_call_target="tpu_custom_call" | custom-call | tf_op jit(solution)/shard_map/sinkhorn/pallas_call | solution.py:471
  141.5 0.0 copy-done.2
  141.5 1.5 %multiply_add_fusion = (f32[512,512]{1,0:T(8,128)}, f32[512,512]{1,0:T(8,128)}) fusion(f32[512,512]{1,0:T(8,128)S(1)} %sinkhorn.1, f32[512,512]{1,0:T(8,128)S(1)} %copy-done, f32[512]{0:T(512)S(1)} %copy-done.2, f32[512]{0:T(512)S(1)} %broadcast_subtract_fusion), kind=kLoop, calls=%fused_computation | loop fusion | flops 1048576 | bytes 4198400 | tf_op jit(solution)/shard_map/add | solution.py:493
Async XLA Ops:
  1.3 1.2 copy-start
  2.5 1.0 copy-start.1
  3.6 137.9 %copy-start.2 = (f32[512]{0:T(512)S(1)}, f32[512]{0:T(512)}, u32[]{:S(2)}) copy-start(f32[512]{0:T(512)} %param.5) | copy-start | bytes 6148

commit v3 on v2

--- a/solution.py
+++ b/solution.py
@@ -18,6 +18,9 @@
 LANES = 128
 X_FIRST = 288
 Y_FIRST = ROWS - X_FIRST
+SPLIT = 704
+PARTS = ((0, SPLIT // 2), (SPLIT // 2, SPLIT // 2), (SPLIT, COLS - SPLIT),
+         (SPLIT, (COLS - SPLIT) // 2), ((COLS + SPLIT) // 2, (COLS - SPLIT) // 2))
 
 
 def log2sumexp2(values):
@@ -28,7 +31,7 @@
 
 def kernel(noise_hbm, data_hbm, out_ref,
            noise_ref, data_ref, load_sem,
-           nb, db, scores, plan, x_parts, x_got, y_parts, y_got, y_sum, lane_lse, noise_col, weight_col, data_row, sq_n, sq_d,
+           nb, db, scores, plan, x_parts, x_got, y_parts, y_got, y_sum, lane_lse, noise_col, weight_col, data_row, top_col, sum_col, sq_n, sq_d,
            row_x, col_x, pair_x,
            n_send, n_recv, d_send, d_recv, s_send, s_recv,
            rx_send, rx_recv, cx_send, cx_recv, px_send, px_recv, m_send, m_recv):
@@ -56,19 +59,12 @@
     load_data.start()
     load_noise.start()
 
+    up, down, mate_chip = at_z(1), at_z(-1), at_z(0, True)
+    right, left, mate_col = at_x(1), at_x(-1), at_x(0, True)
     barrier = pltpu.get_barrier_semaphore()
-    pl.semaphore_signal(barrier, inc=1, device_id=sibling, device_id_type=MESH)
-
-    def greet_col(k, _):
-        pl.semaphore_signal(barrier, inc=1, device_id=(row, lax.rem(col + k, 8)), device_id_type=MESH)
-        return 0
-
-    def greet_row(k, _):
-        pl.semaphore_signal(barrier, inc=1, device_id=(row_peer(k) * 2 + core, col), device_id_type=MESH)
-        return 0
-
-    lax.fori_loop(0, 15, greet_row, 0)
-    lax.fori_loop(1, 8, greet_col, 0)
+    for peer in [sibling] + [(row, c) for c in (right, left, mate_col)] + [
+            (c * 2 + core, col) for c in (up, down, mate_chip)]:
+        pl.semaphore_signal(barrier, inc=1, device_id=peer, device_id_type=MESH)
 
     halfway = pl.ds(pl.multiple_of(core * LANES, LANES), LANES)
     load_data.wait()
@@ -79,146 +75,210 @@
     scores[...] = jnp.zeros_like(scores)
     sq_n[...] = jnp.zeros_like(sq_n)
     sq_d[...] = jnp.zeros_like(sq_d)
-    pl.semaphore_wait(barrier, 23)
+    pl.semaphore_wait(barrier, 7)
 
     sends = []
 
-    def send_noise(chunk, to_col):
-        copy = pltpu.make_async_remote_copy(
-            nb.at[pl.ds(2 * chunk, 2)], nb.at[pl.ds(2 * chunk, 2)],
-            n_send.at[len([s for s in sends if s[0] == "n"])], n_recv.at[chunk],
-            device_id=(row, to_col), device_id_type=MESH)
+    def start(kind, copy):
         copy.start()
-        sends.append(("n", copy))
-
-    def wait_noise(chunk):
-        pltpu.make_async_remote_copy(
-            nb.at[pl.ds(2 * chunk, 2)], nb.at[pl.ds(2 * chunk, 2)], n_send.at[0], n_recv.at[chunk],
-            device_id=(row, col), device_id_type=MESH).wait_recv()
-
-    def send_data(q, to_chip):
-        copy = pltpu.make_async_remote_copy(
-            db.at[q, :, halfway], db.at[q, :, halfway],
-            d_send.at[len([s for s in sends if s[0] == "d"])], d_recv.at[q],
+        sends.append((kind, copy))
+
+    def number(kind):
+        return len([s for s in sends if s[0] == kind])
+
+    def noise_copy(chunk, h, send_at, to_col):
+        piece = nb.at[2 * chunk + h]
+        return pltpu.make_async_remote_copy(
+            piece, piece, n_send.at[send_at], n_recv.at[chunk, h], device_id=(row, to_col), device_id_type=MESH)
+
+    def send_noise(chunk, h, *to_cols):
+        for to_col in to_cols:
+            start("n", noise_copy(chunk, h, number("n"), to_col))
+
+    def wait_noise(chunk, h):
+        noise_copy(chunk, h, 0, col).wait_recv()
+
+    def data_copy(q, part, send_at, to_chip):
+        first, size = PARTS[part]
+        piece = db.at[q, first:first + size, halfway]
+        return pltpu.make_async_remote_copy(
+            piece, piece, d_send.at[send_at], d_recv.at[q, part],
             device_id=(to_chip * 2 + core, col), device_id_type=MESH)
-        copy.start()
-        sends.append(("d", copy))
+
+    def send_data(q, part, *to_chips):
+        for to_chip in to_chips:
+            start("d", data_copy(q, part, number("d"), to_chip))
+
+    def wait_data(q, part):
+        data_copy(q, part, 0, chip).wait_recv()
+
+    def sibling_copy(q, lanes, send_at):
+        return pltpu.make_async_remote_copy(
+            db.at[q, :, lanes], db.at[q, :, lanes], s_send.at[send_at], s_recv.at[q],
+            device_id=sibling, device_id_type=MESH)
 
     def send_sibling(q):
-        copy = pltpu.make_async_remote_copy(
-            db.at[q, :, halfway], db.at[q, :, halfway],
-            s_send.at[len([s for s in sends if s[0] == "s"])], s_recv.at[q],
-            device_id=sibling, device_id_type=MESH)
-        copy.start()
-        sends.append(("s", copy))
-
-    def wait_data(q):
-        pltpu.make_async_remote_copy(
-            db.at[q, :, halfway], db.at[q, :, halfway], d_send.at[0], d_recv.at[q],
-            device_id=sibling, device_id_type=MESH).wait_recv()
+        start("s", sibling_copy(q, halfway, number("s")))
 
     otherway = pl.ds(pl.multiple_of((1 - core) * LANES, LANES), LANES)
 
     def wait_sibling(q):
-        pltpu.make_async_remote_copy(
-            db.at[q, :, otherway], db.at[q, :, otherway], s_send.at[0], s_recv.at[q],
-            device_id=sibling, device_id_type=MESH).wait_recv()
-
-    def pass_data(q, forward):
-        wait_data(q)
-        for shift in forward:
-            send_data(q, at_z(shift))
-        send_sibling(q)
-
-    def level(c):
-        ahead = lax.rem(2 * lax.rem(c, 4) - z + 8, 8)
-        after = lax.rem(ahead + 1, 8)
-        far = jnp.maximum(jnp.minimum(ahead, 8 - ahead), jnp.minimum(after, 8 - after))
-        shift = lax.rem(c // 2 - x + 4, 4)
-        late = jnp.logical_and(lax.rem(shift, 2) == 1, lax.rem(c, 2) != ylo)
-        return jnp.where(far == 4, 4, jnp.where(shift == 2, 3, jnp.where(jnp.logical_or(far == 3, late), 2, 1)))
+        sibling_copy(q, otherway, 0).wait_recv()
+
+    def own_rest(shift):
+        for q, on, end in ((at_z(-shift), up, 3), (at_z(shift), down, 4)):
+            wait_data(q, 2)
+            send_data(q, 2 if shift < 3 else end, on)
+            send_data(q, 2, mate_chip)
+
+    def own_data(shift):
+        for part in (0, 1):
+            wait_data(at_z(-shift), part)
+            send_data(at_z(-shift), part, up)
+            wait_data(at_z(shift), part)
+            if shift < 3:
+                send_data(at_z(shift), part, down)
+        send_sibling(at_z(-shift))
+        send_sibling(at_z(shift))
+
+    def mate_data(shift):
+        for part in (0, 1):
+            wait_data(at_z(-shift, True), part)
+            if shift < 3:
+                send_data(at_z(-shift, True), part, up)
+            wait_data(at_z(shift, True), part)
+            send_data(at_z(shift, True), part, down)
+
+    def mate_rest(*shifts):
+        for shift in shifts:
+            wait_data(at_z(shift, True), 2)
+            send_sibling(at_z(shift, True))
+
+    def data_level(q):
+        ahead = lax.rem(lax.rem(q, 8) - z + 8, 8)
+        far = jnp.minimum(ahead, 8 - ahead)
+        own = q // 8 == yhi
+        return jnp.where(far == 4, 6, jnp.where(far == 3, jnp.where(own, 4, 5),
+                         jnp.where(far == 2, jnp.where(own, 2, 3), jnp.where(jnp.logical_and(own, far == 0), 1, 2))))
+
+    def noise_level(q):
+        shift = lax.rem(q // 4 - x + 4, 4)
+        mate = lax.rem(q // 2, 2) != ylo
+        late = jnp.where(jnp.logical_and(mate, shift >= 2), jnp.where(lax.rem(q, 2) == 0, 4, 6), 3)
+        return jnp.where(jnp.logical_or(shift == 2, jnp.logical_and(mate, shift > 0)), late,
+                         jnp.where(shift == 0, 1, 2))
 
     def multiply(now):
-        def chunk(c, _):
-            @pl.when(level(c) == now)
+        def block(q, _):
+            data_at, noise_at = data_level(q), noise_level(q)
+
+            @pl.when(data_at == now)
             def _():
-                total = scores[...]
-                for h in range(2):
-                    total += lax.dot_general(
-                        nb[2 * c + h], db[2 * c + h], (((1,), (1,)), ((), ())), preferred_element_type=jnp.float32)
-                scores[...] = total
-
-                def data_norm(t, _):
+                def strip(t, _):
                     at = pl.ds(pl.multiple_of(t * LANES, LANES), LANES)
-                    squares = sq_d[at, :]
-                    for h in range(2):
-                        wide = db[2 * c + h, at, :].astype(jnp.float32)
-                        wide = wide * wide
-                        squares = squares + (wide[:, :LANES] + wide[:, LANES:])
-                    sq_d[at, :] = squares
+                    wide = db[q, at, :].astype(jnp.float32)
+                    wide = wide * wide
+                    sq_d[at, :] += wide[:, :LANES] + wide[:, LANES:]
                     return 0
-
-                def noise_norm(t, _):
+                lax.fori_loop(0, COLS // LANES, strip, 0)
+
+            @pl.when(noise_at == now)
+            def _():
+                def strip(t, _):
                     at = pl.ds(pl.multiple_of(t * LANES, LANES), LANES)
-                    squares = sq_n[at, :]
-                    for h in range(2):
-                        wide = nb[2 * c + h, at, :].astype(jnp.float32)
-                        wide = wide * wide
-                        squares = squares + (wide[:, :LANES] + wide[:, LANES:])
-                    sq_n[at, :] = squares
+                    wide = nb[q, at, :].astype(jnp.float32)
+                    wide = wide * wide
+                    sq_n[at, :] += wide[:, :LANES] + wide[:, LANES:]
                     return 0
-
-                lax.fori_loop(0, COLS // LANES, data_norm, 0)
-                lax.fori_loop(0, ROWS // LANES, noise_norm, 0)
-            return 0
-        lax.fori_loop(0, 8, chunk, 0)
-
-    send_data(chip, at_z(0, True))
-    send_data(chip, at_z(1))
-    send_data(chip, at_z(-1))
-    send_noise(col, at_x(0, True))
-    send_noise(col, at_x(1))
-    send_noise(col, at_x(-1))
+                lax.fori_loop(0, ROWS // LANES, strip, 0)
+
+            @pl.when(jnp.maximum(noise_at, data_at) == now)
+            def _():
+                scores[...] += lax.dot_general(
+                    nb[q], db[q], (((1,), (1,)), ((), ())), preferred_element_type=jnp.float32)
+            return 0
+
+        lax.fori_loop(0, QS, block, 0)
+
+    def arrive(*shifts):
+        for shift in shifts:
+            wait_sibling(at_z(shift))
+
+    def mate_arrive(*shifts):
+        for shift in shifts:
+            wait_sibling(at_z(shift, True))
+
+    send_data(chip, 0, mate_chip)
+    send_data(chip, 1, mate_chip)
+    send_data(chip, 2, up, down)
+    for h in (0, 1):
+        send_noise(col, h, right, left, mate_col)
+    send_data(chip, 0, up, down)
+    send_data(chip, 1, up, down)
+    send_data(chip, 2, mate_chip)
     send_sibling(chip)
 
-    pass_data(at_z(-1), (1,))
-    pass_data(at_z(1), (-1,))
-    pass_data(at_z(0, True), (1, -1))
-    wait_noise(at_x(-1))
-    send_noise(at_x(-1), at_x(1))
-    wait_noise(at_x(1))
-    wait_noise(at_x(0, True))
-    send_noise(at_x(0, True), at_x(1))
-    send_noise(at_x(0, True), at_x(-1))
-    pass_data(at_z(-1, True), (1,))
-    pass_data(at_z(1, True), (-1,))
-    pass_data(at_z(-2), (1,))
-    pass_data(at_z(2), (-1,))
-    pass_data(at_z(-2, True), (1,))
-    pass_data(at_z(2, True), (-1,))
-    for shift in (0, 1, -1, 2, -2):
-        wait_sibling(at_z(shift))
-        wait_sibling(at_z(shift, True))
+    own_rest(1)
+    own_data(1)
+    for part in (0, 1):
+        wait_data(mate_chip, part)
+        send_data(mate_chip, part, up, down)
+    wait_noise(left, 0)
+    send_noise(left, 0, right)
+    wait_noise(right, 0)
+    wait_noise(mate_col, 0)
+    send_noise(mate_col, 0, left)
+    own_rest(2)
+    wait_noise(left, 1)
+    send_noise(left, 1, right)
+    wait_noise(right, 1)
+    wait_noise(mate_col, 1)
+    send_noise(mate_col, 1, left)
+    wait_sibling(chip)
     multiply(1)
-    pass_data(at_z(-3), (1,))
-    pass_data(at_z(3), ())
-    wait_noise(at_x(1, True))
-    send_noise(at_x(1, True), at_x(-1))
-    wait_noise(at_x(-1, True))
-    pass_data(at_z(-3, True), ())
-    pass_data(at_z(3, True), (-1,))
-    for shift in (3, -3):
-        wait_sibling(at_z(shift))
-        wait_sibling(at_z(shift, True))
+    own_data(2)
+    mate_data(1)
+    send_noise(mate_col, 0, right)
+    send_noise(mate_col, 1, right)
+    own_rest(3)
+    mate_rest(0, -1, 1)
+    arrive(1, -1, 2, -2)
+    mate_arrive(0, 1, -1)
     multiply(2)
-    wait_noise(at_x(2))
-    wait_noise(at_x(2, True))
+    wait_noise(at_x(1, True), 0)
+    send_noise(at_x(1, True), 0, left)
+    wait_noise(at_x(2), 0)
+    own_data(3)
+    mate_data(2)
+    wait_noise(at_x(1, True), 1)
+    send_noise(at_x(1, True), 1, left)
+    wait_noise(at_x(2), 1)
+    mate_rest(-2, 2)
+    mate_arrive(2, -2)
     multiply(3)
-    pass_data(at_z(4), ())
-    pass_data(at_z(4, True), ())
-    wait_sibling(at_z(4))
-    wait_sibling(at_z(4, True))
+    far, far_mate = at_z(4), at_z(4, True)
+    for part in (3, 4):
+        wait_data(far, part)
+        send_data(far, part, mate_chip)
+    wait_noise(at_x(-1, True), 0)
+    wait_noise(at_x(2, True), 0)
+    arrive(3, -3)
+    mate_data(3)
     multiply(4)
+    mate_rest(-3, 3)
+    mate_arrive(3, -3)
+    multiply(5)
+    wait_data(far, 0)
+    wait_data(far, 1)
+    send_sibling(far)
+    for part in (3, 4, 0, 1):
+        wait_data(far_mate, part)
+    send_sibling(far_mate)
+    wait_noise(at_x(-1, True), 1)
+    wait_noise(at_x(2, True), 1)
+    arrive(4)
+    mate_arrive(4)
+    multiply(6)
 
     scale = LOG2E / (entropic_epsilon * D)
 
@@ -256,7 +316,7 @@
                 sums = sums + jnp.exp2(term - largest)
             lane_lse[at, :] = largest + jnp.log(sums) * LOG2E
             return 0
-        lax.fori_loop(0, ROWS // group, pass_over, 0)
+        lax.fori_loop(0, ROWS // group, pass_over, 0, unroll=2)
         for b in range(ROWS // LANES):
             at = slice(b * LANES, (b + 1) * LANES)
             row_x[e, pl.ds(col, 1), :, at] = log2sumexp2(lane_lse[at, :].T)[None]
@@ -280,14 +340,21 @@
     def data_step(e):
         def pass_over(t, _):
             at = pl.ds(pl.multiple_of(t * LANES, LANES), LANES)
-            partial = []
+            largest, sums = [], []
             for h in range(2):
                 rows = slice(h * 256, (h + 1) * 256)
                 terms = (scores[rows, at] + noise_col[rows, :]).reshape(32, 8, LANES)
-                partial.append(log2sumexp2(terms)[0])
-            pair_x[e, 0, :, at] = log2sumexp2(jnp.concatenate(partial, axis=0))
-            return 0
-        lax.fori_loop(0, COLS // LANES, pass_over, 0)
+                largest.append(jnp.max(terms, axis=0))
+                sums.append(jnp.sum(jnp.exp2(terms - largest[h][None]), axis=0))
+            both = jnp.maximum(*largest)
+            top_col[:, at] = both
+            sum_col[:, at] = sums[0] * jnp.exp2(largest[0] - both) + sums[1] * jnp.exp2(largest[1] - both)
+            return 0
+        lax.fori_loop(0, COLS // LANES, pass_over, 0, unroll=2)
+        tops = top_col[...]
+        whole = jnp.max(tops, axis=0, keepdims=True)
+        sums = jnp.sum(sum_col[...] * jnp.exp2(tops - whole), axis=0, keepdims=True)
+        pair_x[e, 0] = whole + jnp.log(sums) * LOG2E
         swap = pltpu.make_async_remote_copy(
             pair_x.at[e, 0], pair_x.at[e, 1], px_send.at[e], px_recv.at[e],
             device_id=sibling, device_id_type=MESH)
@@ -373,8 +440,6 @@
             y_parts.at[4, :, at, :], y_got.at[4, :, at, :], m_send.at[14 + which], m_recv.at[14 + which],
             device_id=(row, to_col), device_id_type=MESH)
 
-    right, left = at_x(1), at_x(-1)
-    mate_col = at_x(0, True)
     x_copies = [x_copy(slot, to) for slot, to in enumerate((right, left, right, left, right, left, mate_col))]
     y_copies = {slot: y_copy(slot, to) for slot, to in ((0, mate_col), (1, mate_col), (2, mate_col), (3, mate_col), (5, right), (6, left))}
     y_halves = [y_half(0, right), y_half(1, left)]
@@ -471,26 +536,26 @@
     matched = pl.pallas_call(
         kernel,
         out_shape=jax.ShapeDtypeStruct((ROWS, 2 * QW), f32),
-        in_specs=[pl.BlockSpec(memory_space=pl.ANY)] * 2,
+        in_specs=[pl.BlockSpec(memory_space=pltpu.HBM)] * 2,
         out_specs=pl.BlockSpec(memory_space=pltpu.VMEM),
         scratch_shapes=[
             vmem((ROWS, 2 * QW), f32), vmem((COLS, LANES), f32), dma((2,)),
             vmem((QS, ROWS, QW), bf16), vmem((QS, COLS, QW), bf16), vmem((ROWS, COLS), f32), vmem((ROWS, COLS), bf16),
             vmem((7, 2, X_FIRST, QW), bf16), vmem((7, 2, X_FIRST, QW), bf16),
             vmem((7, 2, Y_FIRST, QW), bf16), vmem((7, 2, Y_FIRST, QW), bf16), vmem((2, Y_FIRST, QW), f32),
-            vmem((ROWS, LANES), f32), vmem((ROWS, LANES), f32), vmem((4, ROWS, LANES), f32), vmem((1, COLS), f32),
+            vmem((ROWS, LANES), f32), vmem((ROWS, LANES), f32), vmem((4, ROWS, LANES), f32), vmem((1, COLS), f32), vmem((8, COLS), f32), vmem((8, COLS), f32),
             vmem((ROWS, LANES), f32), vmem((COLS, LANES), f32),
             vmem((SWEEPS + 1, 8, 1, ROWS), f32), vmem((SWEEPS, QS, 1, COLS), f32), vmem((SWEEPS, 2, 1, COLS), f32),
-            dma((8,)), dma((8,)), dma((16,)), dma((16,)), dma((16,)), dma((16,)),
+            dma((14,)), dma((8, 2)), dma((48,)), dma((16, 5)), dma((16,)), dma((16,)),
             dma((SWEEPS + 1, 8)), dma((SWEEPS + 1, 8)), dma((SWEEPS, 16)), dma((SWEEPS, 16)),
             dma((SWEEPS,)), dma((SWEEPS,)), dma((16,)), dma((16,)),
         ],
         compiler_params=pltpu.CompilerParams(
-            collective_id=0, has_side_effects=True, vmem_limit_bytes=48 << 20),
+            collective_id=0, has_side_effects=True, vmem_limit_bytes=60 << 20),
         name="sinkhorn",
     )(noise_latents, data_latents)
     velocity = matched - noise_latents
-    interpolant = (1.0 - flow_times)[:, None] * noise_latents + flow_times[:, None] * matched
+    interpolant = noise_latents + flow_times[:, None] * velocity
     return (velocity, interpolant)
 
 

time: 144 us -> 135 us (0.938)
  Pallas kernels: 138 us -> 131 us
  local copies, waits for them, and re-layouts: 2.27 us -> 0.01 us
    pallas_call x1, Pallas kernels: 138 us -> 131 us  [local(): pl.pallas_call(kernel, out_shape=jax.ShapeDtypeStruct((ROWS, 2 * QW), f32...]
    unnamed x6 -> x4, local copies, waits for them, and re-layouts: 2.27 us -> 0.01 us
where the time goes in v3:
time: 135 us
  Pallas kernels  131 us (97%)
  other arithmetic  2.74 us (2%)
    pallas_call x1, Pallas kernels, local(): pl.pallas_call(kernel, out_shape=jax.ShapeDtypeStruct((ROWS, 2 * QW), f32...  131 us
    add x1, other arithmetic, local(): interpolant = noise_latents + flow_times[:, None] * velocity  2.74 us

profile of v3, /device:TPU:1, one launch (start us, length us, event | category | flops | bytes accessed | tf_op | source)
XLA Modules:
  0.0 134.8 jit_solution(10372610692152204667)
XLA Ops:
  0.6 0.0 copy-start
  0.6 0.0 copy-start.1
  0.6 131.4 %sinkhorn.1 = f32[512,512]{1,0:T(8,128)} custom-call(f32[512,512]{1,0:T(8,128)} %noise_hbm.1, f32[1024,128]{1,0:T(8,128)} %data_hbm.1), custom_call_target="tpu_custom_call" | custom-call | tf_op jit(solution)/shard_map/sinkhorn/pallas_call | solution.py:536
  132.1 0.0 copy-done
  132.1 0.0 copy-done.1
  132.1 2.7 %multiply_add_fusion = (f32[512,512]{1,0:T(8,128)}, f32[512,512]{1,0:T(8,128)}) fusion(f32[512,512]{1,0:T(8,128)S(1)} %copy-done, f32[512]{0:T(512)S(1)} %copy-done.1, f32[512,512]{1,0:T(8,128)} %sinkhorn.1), kind=kLoop, calls=%fused_computation | loop fusion | flops 786432 | bytes 4196352 | tf_op jit(solution)/shard_map/add | solution.py:558
Async XLA Ops:
  0.6 131.4 %copy-start = (f32[512,512]{1,0:T(8,128)S(1)}, f32[512,512]{1,0:T(8,128)}, u32[]{:S(2)}) copy-start(f32[512,512]{1,0:T(8,128)} %noise_hbm.1) | copy-start | bytes 3145732
  0.6 131.4 %copy-start.1 = (f32[512]{0:T(512)S(1)}, f32[512]{0:T(512)}, u32[]{:S(2)}) copy-start(f32[512]{0:T(512)} %param.5) | copy-start | bytes 6148

commit v4 on v3

v4 whole, which is shorter than its diff:
```python
import math

import jax
import jax.numpy as jnp
from jax import lax
from jax.experimental import pallas as pl
from jax.experimental.pallas import tpu as pltpu
from jax.sharding import PartitionSpec as P

D = 4096
SWEEPS = 3
entropic_epsilon = 0.02
MESH = pl.DeviceIdType.MESH
LOG2E = 1.0 / math.log(2.0)

ROWS, COLS = 512, 1024
QS, QW = 16, 256
LANES = 128
COL_ORDER = (4, 3, 5, 2, 6, 1, 7)
X_FIRST = 288
Y_FIRST = ROWS - X_FIRST
SPLIT = 640
PARTS = ((0, SPLIT // 2), (SPLIT // 2, SPLIT // 2), (SPLIT, COLS - SPLIT),
         (SPLIT, (COLS - SPLIT) // 2), ((COLS + SPLIT) // 2, (COLS - SPLIT) // 2), (0, COLS))
WHOLE = 5


def log2sumexp2(values):
    largest = jnp.max(values, axis=0, keepdims=True)
    sums = jnp.sum(jnp.exp2(values - largest), axis=0, keepdims=True)
    return largest + jnp.log(sums) * LOG2E


def kernel(noise_hbm, data_hbm, out_ref,
           noise_ref, data_ref, load_sem,
           nb, db, scores, plan, x_parts, x_got, y_parts, y_got, y_sum, lane_lse, noise_col, weight_col, data_row, top_col, sum_col, sq_n, sq_d,
           row_x, col_x, pair_x,
           n_send, n_recv, d_send, d_recv, s_send, s_recv,
           rx_send, rx_recv, cx_send, cx_recv, px_send, px_recv, m_send, m_recv):
    row, col = lax.axis_index("row"), lax.axis_index("col")
    yhi, z, core = row // 16, lax.rem(row // 2, 8), lax.rem(row, 2)
    x, ylo = col // 2, lax.rem(col, 2)
    chip = row // 2

    def at_x(shift, other=False):
        return lax.rem(x + shift + 4, 4) * 2 + (1 - ylo if other else ylo)

    def at_z(shift, other=False):
        return (1 - yhi if other else yhi) * 8 + lax.rem(z + shift + 8, 8)

    def away(k):
        return (4 + (k + 1) // 2 if k % 2 else 4 - k // 2) % 8

    def row_peer(k):
        return (1 - yhi if k < 8 else yhi) * 8 + lax.rem(z + away(k % 8), 8)

    sibling = (row + 1 - 2 * core, col)
    load_noise = pltpu.make_async_copy(noise_hbm, noise_ref, load_sem.at[0])
    load_data = pltpu.make_async_copy(data_hbm, data_ref, load_sem.at[1])
    load_data.start()
    load_noise.start()

    up, down, mate_chip = at_z(1), at_z(-1), at_z(0, True)
    right, left, mate_col = at_x(1), at_x(-1), at_x(0, True)
    barrier = pltpu.get_barrier_semaphore()
    for peer in [sibling] + [(row, c) for c in (right, left, mate_col)] + [
            (c * 2 + core, col) for c in (up, down, mate_chip)]:
        pl.semaphore_signal(barrier, inc=1, device_id=peer, device_id_type=MESH)

    halfway = pl.ds(pl.multiple_of(core * LANES, LANES), LANES)
    load_data.wait()
    db[chip, :, halfway] = data_ref[...].astype(jnp.bfloat16)
    pl.semaphore_wait(barrier, 7)

    sends = []

    def start(kind, copy):
        copy.start()
        sends.append((kind, copy))

    def number(kind):
        return len([s for s in sends if s[0] == kind])

    def noise_copy(chunk, h, send_at, to_col):
        piece = nb.at[2 * chunk + h]
        return pltpu.make_async_remote_copy(
            piece, piece, n_send.at[send_at], n_recv.at[chunk, h], device_id=(row, to_col), device_id_type=MESH)

    def send_noise(chunk, h, *to_cols):
        for to_col in to_cols:
            start("n", noise_copy(chunk, h, number("n"), to_col))

    def wait_noise(chunk, h):
        noise_copy(chunk, h, 0, col).wait_recv()

    def data_copy(q, part, send_at, to_chip):
        first, size = PARTS[part]
        piece = db.at[q, first:first + size, halfway]
        return pltpu.make_async_remote_copy(
            piece, piece, d_send.at[send_at], d_recv.at[q, part],
            device_id=(to_chip * 2 + core, col), device_id_type=MESH)

    def send_data(q, part, *to_chips):
        for to_chip in to_chips:
            start("d", data_copy(q, part, number("d"), to_chip))

    def wait_data(q, part):
        data_copy(q, part, 0, chip).wait_recv()

    def sibling_copy(q, part, lanes, send_at):
        first, size = PARTS[part]
        piece = db.at[q, first:first + size, lanes]
        return pltpu.make_async_remote_copy(
            piece, piece, s_send.at[send_at], s_recv.at[q, part], device_id=sibling, device_id_type=MESH)

    def send_sibling(q, *parts):
        for part in parts or (WHOLE,):
            start("s", sibling_copy(q, part, halfway, number("s")))

    otherway = pl.ds(pl.multiple_of((1 - core) * LANES, LANES), LANES)

    def wait_sibling(q, *parts):
        for part in parts or (WHOLE,):
            sibling_copy(q, part, otherway, 0).wait_recv()

    def own_rest(shift):
        for q, on, end in ((at_z(-shift), up, 3), (at_z(shift), down, 4)):
            wait_data(q, 2)
            send_data(q, 2 if shift < 3 else end, on)
            send_data(q, 2, mate_chip)

    def own_data(shift):
        for part in (0, 1):
            wait_data(at_z(-shift), part)
            send_data(at_z(-shift), part, up)
            wait_data(at_z(shift), part)
            if shift < 3:
                send_data(at_z(shift), part, down)
        send_sibling(at_z(-shift))
        send_sibling(at_z(shift))

    def mate_data(shift):
        for part in (0, 1):
            wait_data(at_z(-shift, True), part)
            if shift < 3:
                send_data(at_z(-shift, True), part, up)
            wait_data(at_z(shift, True), part)
            send_data(at_z(shift, True), part, down)

    def mate_rest(*shifts):
        for shift in shifts:
            wait_data(at_z(shift, True), 2)
            send_sibling(at_z(shift, True))

    def data_level(q):
        ahead = lax.rem(lax.rem(q, 8) - z + 8, 8)
        far = jnp.minimum(ahead, 8 - ahead)
        return jnp.where(q // 8 == yhi, by_shift(far, (1, 2, 5, 7, 9)), by_shift(far, (3, 4, 6, 8, 9)))

    def by_shift(shift, levels):
        level = levels[-1]
        for at, value in enumerate(levels[:-1]):
            level = jnp.where(shift == at, value, level)
        return level

    def noise_level(q):
        shift, late = lax.rem(q // 4 - x + 4, 4), lax.rem(q, 2) == 1
        return jnp.where(lax.rem(q // 2, 2) == ylo, by_shift(shift, (1, 2, jnp.where(late, 6, 5), 2)),
                         by_shift(shift, (3, jnp.where(late, 6, 5), jnp.where(late, 9, 8))))

    def multiply(now):
        def block(q, _):
            @pl.when(jnp.maximum(noise_level(q), data_level(q)) == now)
            def _():
                for t in range(COLS // QW):
                    at, noise_at = slice(t * QW, (t + 1) * QW), slice(t * LANES, (t + 1) * LANES)
                    scores[:, at] += lax.dot_general(
                        nb[q], db[q, at, :], (((1,), (1,)), ((), ())), preferred_element_type=jnp.float32)
                    wide = db[q, at, :].astype(jnp.float32)
                    wide = wide * wide
                    sq_d[at, :] += wide[:, :LANES] + wide[:, LANES:]
                    wide = nb[q, noise_at, :].astype(jnp.float32)
                    wide = wide * wide
                    sq_n[noise_at, :] += wide[:, :LANES] + wide[:, LANES:]
            return 0

        lax.fori_loop(0, QS, block, 0)

    def arrive(*shifts):
        for shift in shifts:
            wait_sibling(at_z(shift))

    def mate_arrive(*shifts):
        for shift in shifts:
            wait_sibling(at_z(shift, True))

    send_data(chip, 0, mate_chip)
    send_data(chip, 1, mate_chip)
    send_data(chip, 2, up, down)
    load_noise.wait()
    for h in (0, 1):
        nb[2 * col + h] = noise_ref[:, h * QW:(h + 1) * QW].astype(jnp.bfloat16)
        send_noise(col, h, right, left, mate_col)
    send_data(chip, 0, up, down)
    send_data(chip, 1, up, down)
    send_data(chip, 2, mate_chip)
    send_sibling(chip)
    scores[...] = jnp.zeros_like(scores)
    sq_n[...] = jnp.zeros_like(sq_n)
    sq_d[...] = jnp.zeros_like(sq_d)

    own_rest(1)
    own_data(1)
    wait_noise(left, 0)
    send_noise(left, 0, right)
    wait_noise(right, 0)
    for part in (0, 1):
        wait_data(mate_chip, part)
        send_data(mate_chip, part, up, down)
    wait_noise(mate_col, 0)
    send_noise(mate_col, 0, left)
    own_rest(2)
    arrive(0)
    multiply(1)
    wait_noise(left, 1)
    send_noise(left, 1, right)
    wait_noise(right, 1)
    own_data(2)
    mate_rest(0)
    arrive(1, -1)
    multiply(2)
    wait_noise(mate_col, 1)
    send_noise(mate_col, 1, left)
    mate_data(1)
    send_noise(mate_col, 0, right)
    send_noise(mate_col, 1, right)
    own_rest(3)
    mate_rest(-1, 1)
    mate_arrive(0)
    multiply(3)
    wait_noise(at_x(1, True), 0)
    send_noise(at_x(1, True), 0, left)
    wait_noise(at_x(2), 0)
    own_data(3)
    mate_arrive(1, -1)
    multiply(4)
    mate_data(2)
    arrive(2, -2)
    multiply(5)
    wait_noise(at_x(1, True), 1)
    send_noise(at_x(1, True), 1, left)
    wait_noise(at_x(2), 1)
    mate_rest(-2, 2)
    far, far_mate = at_z(4), at_z(4, True)
    for part in (3, 4):
        wait_data(far, part)
        send_data(far, part, mate_chip)
    send_sibling(far, 2)
    mate_arrive(2, -2)
    multiply(6)
    arrive(3, -3)
    multiply(7)
    mate_data(3)
    mate_rest(-3, 3)
    wait_noise(at_x(-1, True), 0)
    wait_noise(at_x(2, True), 0)
    mate_arrive(3, -3)
    multiply(8)
    for part in (0, 1):
        wait_data(far, part)
        send_sibling(far, part)
    for part in (3, 4):
        wait_data(far_mate, part)
    send_sibling(far_mate, 2)
    for part in (0, 1):
        wait_data(far_mate, part)
        send_sibling(far_mate, part)
    wait_noise(at_x(-1, True), 1)
    wait_noise(at_x(2, True), 1)
    wait_sibling(far, 2, 0, 1)
    wait_sibling(far_mate, 2, 0, 1)
    multiply(9)

    scale = LOG2E / (entropic_epsilon * D)

    def norm_row(t, _):
        at = pl.ds(pl.multiple_of(t * LANES, LANES), LANES)
        data_row[:, at] = jnp.sum(sq_d[at, :].T, axis=0, keepdims=True)
        return 0

    lax.fori_loop(0, COLS // LANES, norm_row, 0)
    group = 32

    def to_column(column_ref, line):
        for b in range(ROWS // LANES):
            at = slice(b * LANES, (b + 1) * LANES)
            column_ref[at, :] = jnp.broadcast_to(line[:, at], (LANES, LANES)).T

    def noise_step(e):
        def pass_over(t, _):
            at = pl.ds(pl.multiple_of(t * group, group), group)
            if e == 0:
                norms = jnp.sum(sq_n[at, :], axis=1, keepdims=True)
                terms = []
                for c in range(COLS // LANES):
                    lanes = slice(c * LANES, (c + 1) * LANES)
                    terms.append((2.0 * scores[at, lanes] - norms - data_row[:, lanes]) * scale)
                    scores[at, lanes] = terms[c]
            else:
                terms = [scores[at, c * LANES:(c + 1) * LANES] + data_row[:, c * LANES:(c + 1) * LANES]
                         for c in range(COLS // LANES)]
            largest = terms[0]
            for term in terms[1:]:
                largest = jnp.maximum(largest, term)
            sums = jnp.exp2(terms[0] - largest)
            for term in terms[1:]:
                sums = sums + jnp.exp2(term - largest)
            lane_lse[at, :] = largest + jnp.log(sums) * LOG2E
            return 0
        lax.fori_loop(0, ROWS // group, pass_over, 0, unroll=2)
        for b in range(ROWS // LANES):
            at = slice(b * LANES, (b + 1) * LANES)
            row_x[e, pl.ds(col, 1), :, at] = log2sumexp2(lane_lse[at, :].T)[None]

        for k in COL_ORDER:
            row_copy(e, col, k).start()

    def row_copy(e, source, k):
        return pltpu.make_async_remote_copy(
            row_x.at[e, source], row_x.at[e, source], rx_send.at[e, k], rx_recv.at[e, source],
            device_id=(row, lax.rem(col + k, 8)), device_id_type=MESH)

    def noise_arrives(e):
        for k in COL_ORDER[::-1]:
            row_copy(e, lax.rem(col + k, 8), k).wait_recv()

    def col_copy(e, source, k):
        return pltpu.make_async_remote_copy(
            col_x.at[e, source], col_x.at[e, source], cx_send.at[e, k], cx_recv.at[e, source],
            device_id=(row_peer(k) * 2 + core, col), device_id_type=MESH)

    def swap_copy(e):
        return pltpu.make_async_remote_copy(
            pair_x.at[e, 0], pair_x.at[e, 1], px_send.at[e], px_recv.at[e],
            device_id=sibling, device_id_type=MESH)

    def data_step(e):
        def pass_over(t, _):
            at = pl.ds(pl.multiple_of(t * LANES, LANES), LANES)
            largest, sums = [], []
            for h in range(2):
                rows = slice(h * 256, (h + 1) * 256)
                terms = (scores[rows, at] + noise_col[rows, :]).reshape(32, 8, LANES)
                largest.append(jnp.max(terms, axis=0))
                sums.append(jnp.sum(jnp.exp2(terms - largest[h][None]), axis=0))
            both = jnp.maximum(*largest)
            top_col[:, at] = both
            sum_col[:, at] = sums[0] * jnp.exp2(largest[0] - both) + sums[1] * jnp.exp2(largest[1] - both)
            return 0
        lax.fori_loop(0, COLS // LANES, pass_over, 0, unroll=2)
        tops = top_col[...]
        whole = jnp.max(tops, axis=0, keepdims=True)
        sums = jnp.sum(sum_col[...] * jnp.exp2(tops - whole), axis=0, keepdims=True)
        pair_x[e, 0] = whole + jnp.log(sums) * LOG2E
        swap = swap_copy(e)
        swap.start()
        swap.wait_recv()
        col_x[e, pl.ds(chip, 1)] = log2sumexp2(pair_x[e])

        for k in range(15):
            col_copy(e, chip, k).start()
        for k in range(14, -1, -1):
            col_copy(e, row_peer(k), k).wait_recv()
        data_row[...] = -log2sumexp2(col_x[e])[0] - math.log2(8192)

    for e in range(SWEEPS):
        noise_step(e)
        noise_arrives(e)
        to_column(noise_col, -log2sumexp2(row_x[e])[0] - math.log2(16384))
        data_step(e)

    noise_step(SWEEPS)
    to_column(noise_col, row_x[SWEEPS, col])

    def transport(t, _):
        at = pl.ds(pl.multiple_of(t * group, group), group)
        for c in range(COLS // LANES):
            lanes = slice(c * LANES, (c + 1) * LANES)
            plan[at, lanes] = jnp.exp2(data_row[:, lanes] + scores[at, lanes] - noise_col[at, :]).astype(jnp.bfloat16)
        return 0

    lax.fori_loop(0, ROWS // group, transport, 0)

    top, low = slice(0, X_FIRST), slice(X_FIRST, ROWS)
    half = Y_FIRST // 2
    SELF, LEFT, RIGHT, MATE = range(4)

    def chunk_sum(rows, target, h):
        return jnp.dot(plan[rows, :], db[2 * target + h], preferred_element_type=jnp.float32)

    def weigh(value, who, rows):
        weight = weight_col[who, rows, :]
        return jnp.concatenate([value[:, :LANES] * weight, value[:, LANES:] * weight], axis=1)

    def fill(ref, slot, h, rows, target, add=(), weighed=True):
        value = chunk_sum(rows, target, h)
        if weighed:
            value = weigh(value, SELF, rows)
        for other, other_slot, who in add:
            term = other[other_slot, h].astype(jnp.float32)
            value = value + (term if who is None else weigh(term, who, rows))
        ref[slot, h] = value.astype(jnp.bfloat16)

    def x_copy(slot, h, to_col):
        return pltpu.make_async_remote_copy(
            x_parts.at[slot, h], x_got.at[slot, h], m_send.at[slot, h], m_recv.at[slot, h],
            device_id=(row, to_col), device_id_type=MESH)

    def y_copy(slot, h, to_col):
        return pltpu.make_async_remote_copy(
            y_parts.at[slot, h], y_got.at[slot, h], m_send.at[7 + slot, h], m_recv.at[7 + slot, h],
            device_id=(row, to_col), device_id_type=MESH)

    def y_half(which, h, to_col):
        at = pl.ds(which * half, half)
        return pltpu.make_async_remote_copy(
            y_parts.at[4, h, at, :], y_got.at[4, h, at, :], m_send.at[14 + which, h], m_recv.at[14 + which, h],
            device_id=(row, to_col), device_id_type=MESH)

    x_copies = [[x_copy(slot, h, to) for h in range(2)]
                for slot, to in enumerate((right, left, right, left, right, left, mate_col))]
    y_copies = {slot: [y_copy(slot, h, to) for h in range(2)]
                for slot, to in ((0, mate_col), (1, mate_col), (2, mate_col), (3, mate_col), (5, right), (6, left))}
    y_halves = [[y_half(which, h, to) for h in range(2)] for which, to in enumerate((right, left))]

    for h in range(2):
        fill(x_parts, 0, h, top, at_x(2), weighed=False)
        x_copies[0][h].start()
        fill(x_parts, 1, h, top, at_x(2, True), weighed=False)
        x_copies[1][h].start()
        fill(y_parts, 0, h, low, at_x(2, True), weighed=False)
        y_copies[0][h].start()
    for slot, target in ((1, at_x(1, True)), (2, at_x(-1, True)), (3, mate_col)):
        for h in range(2):
            fill(y_parts, slot, h, low, target, weighed=False)
            y_copies[slot][h].start()

    noise_arrives(SWEEPS)
    whole = log2sumexp2(row_x[SWEEPS])[0]
    for who, source in enumerate((col, left, right, mate_col)):
        to_column(weight_col.at[who], jnp.exp2(row_x[SWEEPS, source] - whole))

    for h in range(2):
        y_copies[0][h].wait_recv()
        fill(y_parts, 4, h, low, at_x(2), add=[(y_got, 0, MATE)])
        y_halves[0][h].start()
        y_halves[1][h].start()
        x_copies[1][h].wait_recv()
        fill(x_parts, 5, h, top, at_x(-1, True), add=[(x_got, 1, RIGHT)])
        x_copies[5][h].start()
        fill(x_parts, 2, h, top, at_x(1, True))
        x_copies[2][h].start()
    for h in range(2):
        x_copies[0][h].wait_recv()
        fill(x_parts, 4, h, top, right, add=[(x_got, 0, LEFT)])
        x_copies[4][h].start()
        fill(x_parts, 3, h, top, left)
        x_copies[3][h].start()

    def low_sum(target, h, got_slot):
        return (weigh(chunk_sum(low, target, h), SELF, low)
                + weigh(y_got[got_slot, h].astype(jnp.float32), MATE, low))

    for slot, target, got_slot, which in ((5, right, 1, 0), (6, left, 2, 1)):
        at, rest = pl.ds(which * half, half), pl.ds((1 - which) * half, half)
        for h in range(2):
            y_copies[got_slot][h].wait_recv()
            y_sum[...] = low_sum(target, h, got_slot)
            y_parts[slot, h, rest, :] = y_sum[rest, :].astype(jnp.bfloat16)
            y_halves[which][h].wait_recv()
            y_parts[slot, h, at, :] = (y_sum[at, :] + y_got[4, h, at, :].astype(jnp.float32)).astype(jnp.bfloat16)
            y_copies[slot][h].start()

    for h in range(2):
        x_copies[2][h].wait_recv()
        x_copies[5][h].wait_recv()
        fill(x_parts, 6, h, top, mate_col, add=[(x_got, 2, None), (x_got, 5, None)])
        x_copies[6][h].start()
    for h in range(2):
        lanes = slice(h * QW, (h + 1) * QW)
        y_copies[3][h].wait_recv()
        out_ref[low, lanes] = low_sum(col, h, 3)
        out_ref[top, lanes] = weigh(chunk_sum(top, col, h), SELF, top)
    for h in range(2):
        lanes = slice(h * QW, (h + 1) * QW)
        x_copies[3][h].wait_recv()
        x_copies[4][h].wait_recv()
        out_ref[top, lanes] += x_got[3, h].astype(jnp.float32) + x_got[4, h].astype(jnp.float32)
    for h in range(2):
        lanes = slice(h * QW, (h + 1) * QW)
        y_copies[5][h].wait_recv()
        y_copies[6][h].wait_recv()
        out_ref[low, lanes] += y_got[5, h].astype(jnp.float32) + y_got[6, h].astype(jnp.float32)
        x_copies[6][h].wait_recv()
        out_ref[top, lanes] += x_got[6, h].astype(jnp.float32)

    for pair in x_copies + list(y_copies.values()) + y_halves:
        for copy in pair:
            copy.wait_send()
    for e in range(SWEEPS + 1):
        for k in range(1, 8):
            row_copy(e, col, k).wait_send()
    for e in range(SWEEPS):
        for k in range(15):
            col_copy(e, chip, k).wait_send()
        swap_copy(e).wait_send()
    for _, copy in sends:
        copy.wait_send()


def local(noise_latents, data_latents, flow_times):
    bf16, f32 = jnp.bfloat16, jnp.float32
    vmem, dma = pltpu.VMEM, pltpu.SemaphoreType.DMA
    matched = pl.pallas_call(
        kernel,
        out_shape=jax.ShapeDtypeStruct((ROWS, 2 * QW), f32),
        in_specs=[pl.BlockSpec(memory_space=pltpu.HBM)] * 2,
        out_specs=pl.BlockSpec(memory_space=pltpu.VMEM),
        scratch_shapes=[
            vmem((ROWS, 2 * QW), f32), vmem((COLS, LANES), f32), dma((2,)),
            vmem((QS, ROWS, QW), bf16), vmem((QS, COLS, QW), bf16), vmem((ROWS, COLS), f32), vmem((ROWS, COLS), bf16),
            vmem((7, 2, X_FIRST, QW), bf16), vmem((7, 2, X_FIRST, QW), bf16),
            vmem((7, 2, Y_FIRST, QW), bf16), vmem((7, 2, Y_FIRST, QW), bf16), vmem((Y_FIRST, QW), f32),
            vmem((ROWS, LANES), f32), vmem((ROWS, LANES), f32), vmem((4, ROWS, LANES), f32), vmem((1, COLS), f32), vmem((8, COLS), f32), vmem((8, COLS), f32),
            vmem((ROWS, LANES), f32), vmem((COLS, LANES), f32),
            vmem((SWEEPS + 1, 8, 1, ROWS), f32), vmem((SWEEPS, QS, 1, COLS), f32), vmem((SWEEPS, 2, 1, COLS), f32),
            dma((14,)), dma((8, 2)), dma((48,)), dma((16, 5)), dma((20,)), dma((16, 6)),
            dma((SWEEPS + 1, 8)), dma((SWEEPS + 1, 8)), dma((SWEEPS, 16)), dma((SWEEPS, 16)),
            dma((SWEEPS,)), dma((SWEEPS,)), dma((16, 2)), dma((16, 2)),
        ],
        compiler_params=pltpu.CompilerParams(
            collective_id=0, has_side_effects=True, vmem_limit_bytes=60 << 20),
        name="sinkhorn",
    )(noise_latents, data_latents)
    velocity = matched - noise_latents
    interpolant = noise_latents + flow_times[:, None] * velocity
    return (velocity, interpolant)


def solution(mesh):
    in_specs = (P("row", "col"), P("col", "row"), P("row"))
    out_specs = (P("row", "col"), P("row", "col"))
    return jax.shard_map(local, mesh=mesh, in_specs=in_specs, out_specs=out_specs, check_vma=False)
```

time: 135 us -> 130 us (0.963)
  Pallas kernels: 131 us -> 126 us
    pallas_call x1, Pallas kernels: 131 us -> 126 us  [local(): pl.pallas_call(kernel, out_shape=jax.ShapeDtypeStruct((ROWS, 2 * QW), f32...]
where the time goes in v4:
time: 130 us; the launch traced here: 129 us
  Pallas kernels  126 us (97%)
  other arithmetic  2.74 us (2%)
    pallas_call x1, Pallas kernels, local(): pl.pallas_call(kernel, out_shape=jax.ShapeDtypeStruct((ROWS, 2 * QW), f32...  126 us
    add x1, other arithmetic, local(): interpolant = noise_latents + flow_times[:, None] * velocity  2.74 us

profile of v4, /device:TPU:1, one launch (start us, length us, event | category | flops | bytes accessed | tf_op | source)
XLA Modules:
  0.0 129.4 jit_solution(2352067206430777327)
XLA Ops:
  0.6 0.0 copy-start
  0.6 0.0 copy-start.1
  0.6 126.0 %sinkhorn.1 = f32[512,512]{1,0:T(8,128)} custom-call(f32[512,512]{1,0:T(8,128)} %noise_hbm.1, f32[1024,128]{1,0:T(8,128)} %data_hbm.1), custom_call_target="tpu_custom_call" | custom-call | tf_op jit(solution)/shard_map/sinkhorn/pallas_call | solution.py:524
  126.7 0.0 copy-done
  126.7 0.0 copy-done.1
  126.7 2.7 %multiply_add_fusion = (f32[512,512]{1,0:T(8,128)}, f32[512,512]{1,0:T(8,128)}) fusion(f32[512,512]{1,0:T(8,128)S(1)} %copy-done, f32[512]{0:T(512)S(1)} %copy-done.1, f32[512,512]{1,0:T(8,128)} %sinkhorn.1), kind=kLoop, calls=%fused_computation | loop fusion | flops 786432 | bytes 4196352 | tf_op jit(solution)/shard_map/add | solution.py:546
Async XLA Ops:
  0.6 126.0 %copy-start = (f32[512,512]{1,0:T(8,128)S(1)}, f32[512,512]{1,0:T(8,128)}, u32[]{:S(2)}) copy-start(f32[512,512]{1,0:T(8,128)} %noise_hbm.1) | copy-start | bytes 3145732
  0.6 126.0 %copy-start.1 = (f32[512]{0:T(512)S(1)}, f32[512]{0:T(512)}, u32[]{:S(2)}) copy-start(f32[512]{0:T(512)} %param.5) | copy-start | bytes 6148

commit v5 on v4

--- a/solution.py
+++ b/solution.py
@@ -33,7 +33,7 @@
 
 def kernel(noise_hbm, data_hbm, out_ref,
            noise_ref, data_ref, load_sem,
-           nb, db, scores, plan, x_parts, x_got, y_parts, y_got, y_sum, lane_lse, noise_col, weight_col, data_row, top_col, sum_col, sq_n, sq_d,
+           nb, db, scores, plan, x_parts, x_got, y_parts, y_got, y_sum, top_row, sum_row, noise_col, weight_col, data_row, top_col, sum_col, sq_n, sq_d,
            row_x, col_x, pair_x,
            n_send, n_recv, d_send, d_recv, s_send, s_recv,
            rx_send, rx_recv, cx_send, cx_recv, px_send, px_recv, m_send, m_recv):
@@ -132,9 +132,10 @@
     def own_data(shift):
         for part in (0, 1):
             wait_data(at_z(-shift), part)
-            send_data(at_z(-shift), part, up)
+            if shift < 3 or part == 0:
+                send_data(at_z(-shift), part, up)
             wait_data(at_z(shift), part)
-            if shift < 3:
+            if shift < 3 or part == 1:
                 send_data(at_z(shift), part, down)
         send_sibling(at_z(-shift))
         send_sibling(at_z(shift))
@@ -142,10 +143,11 @@
     def mate_data(shift):
         for part in (0, 1):
             wait_data(at_z(-shift, True), part)
-            if shift < 3:
+            if shift < 3 or part == 0:
                 send_data(at_z(-shift, True), part, up)
             wait_data(at_z(shift, True), part)
-            send_data(at_z(shift, True), part, down)
+            if shift < 3 or part == 1:
+                send_data(at_z(shift, True), part, down)
 
     def mate_rest(*shifts):
         for shift in shifts:
@@ -155,7 +157,7 @@
     def data_level(q):
         ahead = lax.rem(lax.rem(q, 8) - z + 8, 8)
         far = jnp.minimum(ahead, 8 - ahead)
-        return jnp.where(q // 8 == yhi, by_shift(far, (1, 2, 5, 7, 9)), by_shift(far, (3, 4, 6, 8, 9)))
+        return jnp.where(q // 8 == yhi, by_shift(far, (1, 2, 5, 7, 10)), by_shift(far, (3, 4, 6, 8, 10)))
 
     def by_shift(shift, levels):
         level = levels[-1]
@@ -259,8 +261,8 @@
     mate_arrive(2, -2)
     multiply(6)
     arrive(3, -3)
+    mate_data(3)
     multiply(7)
-    mate_data(3)
     mate_rest(-3, 3)
     wait_noise(at_x(-1, True), 0)
     wait_noise(at_x(2, True), 0)
@@ -277,9 +279,10 @@
         send_sibling(far_mate, part)
     wait_noise(at_x(-1, True), 1)
     wait_noise(at_x(2, True), 1)
+    multiply(9)
     wait_sibling(far, 2, 0, 1)
     wait_sibling(far_mate, 2, 0, 1)
-    multiply(9)
+    multiply(10)
 
     scale = LOG2E / (entropic_epsilon * D)
 
@@ -315,12 +318,16 @@
             sums = jnp.exp2(terms[0] - largest)
             for term in terms[1:]:
                 sums = sums + jnp.exp2(term - largest)
-            lane_lse[at, :] = largest + jnp.log(sums) * LOG2E
+            top_row[at, :] = largest
+            sum_row[at, :] = sums
             return 0
-        lax.fori_loop(0, ROWS // group, pass_over, 0, unroll=2)
+        lax.fori_loop(0, ROWS // group, pass_over, 0, unroll=4)
         for b in range(ROWS // LANES):
             at = slice(b * LANES, (b + 1) * LANES)
-            row_x[e, pl.ds(col, 1), :, at] = log2sumexp2(lane_lse[at, :].T)[None]
+            tops = top_row[at, :].T
+            whole = jnp.max(tops, axis=0, keepdims=True)
+            sums = jnp.sum(sum_row[at, :].T * jnp.exp2(tops - whole), axis=0, keepdims=True)
+            row_x[e, pl.ds(col, 1), :, at] = (whole + jnp.log(sums) * LOG2E)[None]
 
         for k in COL_ORDER:
             row_copy(e, col, k).start()
@@ -357,7 +364,7 @@
             top_col[:, at] = both
             sum_col[:, at] = sums[0] * jnp.exp2(largest[0] - both) + sums[1] * jnp.exp2(largest[1] - both)
             return 0
-        lax.fori_loop(0, COLS // LANES, pass_over, 0, unroll=2)
+        lax.fori_loop(0, COLS // LANES, pass_over, 0, unroll=4)
         tops = top_col[...]
         whole = jnp.max(tops, axis=0, keepdims=True)
         sums = jnp.sum(sum_col[...] * jnp.exp2(tops - whole), axis=0, keepdims=True)
@@ -389,7 +396,7 @@
             plan[at, lanes] = jnp.exp2(data_row[:, lanes] + scores[at, lanes] - noise_col[at, :]).astype(jnp.bfloat16)
         return 0
 
-    lax.fori_loop(0, ROWS // group, transport, 0)
+    lax.fori_loop(0, ROWS // group, transport, 0, unroll=4)
 
     top, low = slice(0, X_FIRST), slice(X_FIRST, ROWS)
     half = Y_FIRST // 2
@@ -467,6 +474,16 @@
         fill(x_parts, 3, h, top, left)
         x_copies[3][h].start()
 
+    for _, copy in sends:
+        copy.wait_send()
+    for e in range(SWEEPS + 1):
+        for k in COL_ORDER:
+            row_copy(e, col, k).wait_send()
+    for e in range(SWEEPS):
+        for k in range(15):
+            col_copy(e, chip, k).wait_send()
+        swap_copy(e).wait_send()
+
     def low_sum(target, h, got_slot):
         return (weigh(chunk_sum(low, target, h), SELF, low)
                 + weigh(y_got[got_slot, h].astype(jnp.float32), MATE, low))
@@ -491,6 +508,9 @@
         y_copies[3][h].wait_recv()
         out_ref[low, lanes] = low_sum(col, h, 3)
         out_ref[top, lanes] = weigh(chunk_sum(top, col, h), SELF, top)
+    for copies in x_copies[:3] + x_copies[5:6] + [y_copies[slot] for slot in range(4)] + y_halves:
+        for copy in copies:
+            copy.wait_send()
     for h in range(2):
         lanes = slice(h * QW, (h + 1) * QW)
         x_copies[3][h].wait_recv()
@@ -504,18 +524,9 @@
         x_copies[6][h].wait_recv()
         out_ref[top, lanes] += x_got[6, h].astype(jnp.float32)
 
-    for pair in x_copies + list(y_copies.values()) + y_halves:
-        for copy in pair:
+    for copies in (x_copies[3], x_copies[4], x_copies[6], y_copies[5], y_copies[6]):
+        for copy in copies:
             copy.wait_send()
-    for e in range(SWEEPS + 1):
-        for k in range(1, 8):
-            row_copy(e, col, k).wait_send()
-    for e in range(SWEEPS):
-        for k in range(15):
-            col_copy(e, chip, k).wait_send()
-        swap_copy(e).wait_send()
-    for _, copy in sends:
-        copy.wait_send()
 
 
 def local(noise_latents, data_latents, flow_times):
@@ -531,7 +542,7 @@
             vmem((QS, ROWS, QW), bf16), vmem((QS, COLS, QW), bf16), vmem((ROWS, COLS), f32), vmem((ROWS, COLS), bf16),
             vmem((7, 2, X_FIRST, QW), bf16), vmem((7, 2, X_FIRST, QW), bf16),
             vmem((7, 2, Y_FIRST, QW), bf16), vmem((7, 2, Y_FIRST, QW), bf16), vmem((Y_FIRST, QW), f32),
-            vmem((ROWS, LANES), f32), vmem((ROWS, LANES), f32), vmem((4, ROWS, LANES), f32), vmem((1, COLS), f32), vmem((8, COLS), f32), vmem((8, COLS), f32),
+            vmem((ROWS, LANES), f32), vmem((ROWS, LANES), f32), vmem((ROWS, LANES), f32), vmem((4, ROWS, LANES), f32), vmem((1, COLS), f32), vmem((8, COLS), f32), vmem((8, COLS), f32),
             vmem((ROWS, LANES), f32), vmem((COLS, LANES), f32),
             vmem((SWEEPS + 1, 8, 1, ROWS), f32), vmem((SWEEPS, QS, 1, COLS), f32), vmem((SWEEPS, 2, 1, COLS), f32),
             dma((14,)), dma((8, 2)), dma((48,)), dma((16, 5)), dma((20,)), dma((16, 6)),

time: 130 us -> 127 us (0.977)
  Pallas kernels: 126 us -> 123 us
    pallas_call x1, Pallas kernels: 126 us -> 123 us  [local(): pl.pallas_call(kernel, out_shape=jax.ShapeDtypeStruct((ROWS, 2 * QW), f32...]
where the time goes in v5:
time: 127 us
  Pallas kernels  123 us (97%)
  other arithmetic  2.74 us (2%)
    pallas_call x1, Pallas kernels, local(): pl.pallas_call(kernel, out_shape=jax.ShapeDtypeStruct((ROWS, 2 * QW), f32...  123 us
    add x1, other arithmetic, local(): interpolant = noise_latents + flow_times[:, None] * velocity  2.74 us

profile of v5, /device:TPU:1, one launch (start us, length us, event | category | flops | bytes accessed | tf_op | source)
XLA Modules:
  0.0 126.5 jit_solution(14093427732929414807)
XLA Ops:
  0.6 0.0 copy-start
  0.6 0.0 copy-start.1
  0.6 123.1 %sinkhorn.1 = f32[512,512]{1,0:T(8,128)} custom-call(f32[512,512]{1,0:T(8,128)} %noise_hbm.1, f32[1024,128]{1,0:T(8,128)} %data_hbm.1), custom_call_target="tpu_custom_call" | custom-call | tf_op jit(solution)/shard_map/sinkhorn/pallas_call | solution.py:535
  123.8 0.0 copy-done
  123.8 0.0 copy-done.1
  123.8 2.7 %multiply_add_fusion = (f32[512,512]{1,0:T(8,128)}, f32[512,512]{1,0:T(8,128)}) fusion(f32[512,512]{1,0:T(8,128)S(1)} %copy-done, f32[512]{0:T(512)S(1)} %copy-done.1, f32[512,512]{1,0:T(8,128)} %sinkhorn.1), kind=kLoop, calls=%fused_computation | loop fusion | flops 786432 | bytes 4196352 | tf_op jit(solution)/shard_map/add | solution.py:557
Async XLA Ops:
  0.6 123.2 %copy-start = (f32[512,512]{1,0:T(8,128)S(1)}, f32[512,512]{1,0:T(8,128)}, u32[]{:S(2)}) copy-start(f32[512,512]{1,0:T(8,128)} %noise_hbm.1) | copy-start | bytes 3145732
  0.6 123.2 %copy-start.1 = (f32[512]{0:T(512)S(1)}, f32[512]{0:T(512)}, u32[]{:S(2)}) copy-start(f32[512]{0:T(512)} %param.5) | copy-start | bytes 6148

commit v6 on v5

--- a/solution.py
+++ b/solution.py
@@ -17,6 +17,9 @@
 QS, QW = 16, 256
 LANES = 128
 COL_ORDER = (4, 3, 5, 2, 6, 1, 7)
+NEAR = ((1, 2), (1, 6), (0, 4), (1, 1), (1, 7), (0, 3), (0, 5), (1, 0), (0, 2), (0, 6), (0, 1), (0, 7))
+FAR = ((1, 4), (1, 3), (1, 5))
+OWN = len(NEAR)
 X_FIRST = 288
 Y_FIRST = ROWS - X_FIRST
 SPLIT = 640
@@ -47,12 +50,6 @@
 
     def at_z(shift, other=False):
         return (1 - yhi if other else yhi) * 8 + lax.rem(z + shift + 8, 8)
-
-    def away(k):
-        return (4 + (k + 1) // 2 if k % 2 else 4 - k // 2) % 8
-
-    def row_peer(k):
-        return (1 - yhi if k < 8 else yhi) * 8 + lax.rem(z + away(k % 8), 8)
 
     sibling = (row + 1 - 2 * core, col)
     load_noise = pltpu.make_async_copy(noise_hbm, noise_ref, load_sem.at[0])
@@ -341,10 +338,24 @@
         for k in COL_ORDER[::-1]:
             row_copy(e, lax.rem(col + k, 8), k).wait_recv()
 
-    def col_copy(e, source, k):
-        return pltpu.make_async_remote_copy(
-            col_x.at[e, source], col_x.at[e, source], cx_send.at[e, k], cx_recv.at[e, source],
-            device_id=(row_peer(k) * 2 + core, col), device_id_type=MESH)
+    def mirrored(peers, k):
+        return peers.index((peers[k][0], (8 - peers[k][1]) % 8))
+
+    def near_copy(e, k, slot):
+        return pltpu.make_async_remote_copy(
+            col_x.at[e, OWN], col_x.at[e, slot], cx_send.at[e, k], cx_recv.at[e, slot],
+            device_id=(at_z(NEAR[k][1], NEAR[k][0] == 1) * 2 + core, col), device_id_type=MESH)
+
+    def far_copy(e, k, to_core, slot, from_core):
+        slot = OWN + 1 + 2 * slot + from_core
+        return pltpu.make_async_remote_copy(
+            pair_x.at[e, 0], col_x.at[e, slot], cx_send.at[e, OWN + 2 * k + to_core], cx_recv.at[e, slot],
+            device_id=(at_z(FAR[k][1], True) * 2 + to_core, col), device_id_type=MESH)
+
+    def row_sends(e):
+        near = [near_copy(e, k, mirrored(NEAR, k)) for k in range(len(NEAR))]
+        far = [far_copy(e, k, to_core, mirrored(FAR, k), core) for k in range(len(FAR)) for to_core in range(2)]
+        return near, far
 
     def swap_copy(e):
         return pltpu.make_async_remote_copy(
@@ -369,15 +380,19 @@
         whole = jnp.max(tops, axis=0, keepdims=True)
         sums = jnp.sum(sum_col[...] * jnp.exp2(tops - whole), axis=0, keepdims=True)
         pair_x[e, 0] = whole + jnp.log(sums) * LOG2E
-        swap = swap_copy(e)
+        swap, (near, far) = swap_copy(e), row_sends(e)
         swap.start()
+        for copy in far:
+            copy.start()
         swap.wait_recv()
-        col_x[e, pl.ds(chip, 1)] = log2sumexp2(pair_x[e])
-
-        for k in range(15):
-            col_copy(e, chip, k).start()
-        for k in range(14, -1, -1):
-            col_copy(e, row_peer(k), k).wait_recv()
+        col_x[e, OWN] = log2sumexp2(pair_x[e])[0]
+        for copy in near:
+            copy.start()
+        for k in range(len(NEAR) - 1, -1, -1):
+            near_copy(e, k, k).wait_recv()
+        for k in range(len(FAR)):
+            for from_core in range(2):
+                far_copy(e, k, 0, k, from_core).wait_recv()
         data_row[...] = -log2sumexp2(col_x[e])[0] - math.log2(8192)
 
     for e in range(SWEEPS):
@@ -480,8 +495,9 @@
         for k in COL_ORDER:
             row_copy(e, col, k).wait_send()
     for e in range(SWEEPS):
-        for k in range(15):
-            col_copy(e, chip, k).wait_send()
+        for copies in row_sends(e):
+            for copy in copies:
+                copy.wait_send()
         swap_copy(e).wait_send()
 
     def low_sum(target, h, got_slot):
@@ -544,9 +560,9 @@
             vmem((7, 2, Y_FIRST, QW), bf16), vmem((7, 2, Y_FIRST, QW), bf16), vmem((Y_FIRST, QW), f32),
             vmem((ROWS, LANES), f32), vmem((ROWS, LANES), f32), vmem((ROWS, LANES), f32), vmem((4, ROWS, LANES), f32), vmem((1, COLS), f32), vmem((8, COLS), f32), vmem((8, COLS), f32),
             vmem((ROWS, LANES), f32), vmem((COLS, LANES), f32),
-            vmem((SWEEPS + 1, 8, 1, ROWS), f32), vmem((SWEEPS, QS, 1, COLS), f32), vmem((SWEEPS, 2, 1, COLS), f32),
+            vmem((SWEEPS + 1, 8, 1, ROWS), f32), vmem((SWEEPS, OWN + 1 + 2 * len(FAR), 1, COLS), f32), vmem((SWEEPS, 2, 1, COLS), f32),
             dma((14,)), dma((8, 2)), dma((48,)), dma((16, 5)), dma((20,)), dma((16, 6)),
-            dma((SWEEPS + 1, 8)), dma((SWEEPS + 1, 8)), dma((SWEEPS, 16)), dma((SWEEPS, 16)),
+            dma((SWEEPS + 1, 8)), dma((SWEEPS + 1, 8)), dma((SWEEPS, 20)), dma((SWEEPS, 20)),
             dma((SWEEPS,)), dma((SWEEPS,)), dma((16, 2)), dma((16, 2)),
         ],
         compiler_params=pltpu.CompilerParams(

time: 127 us -> 126 us (level)
  no operation moved by 1% of the time
where the time goes in v6:
time: 126 us
  Pallas kernels  122 us (97%)
  other arithmetic  2.74 us (2%)
    pallas_call x1, Pallas kernels, local(): pl.pallas_call(kernel, out_shape=jax.ShapeDtypeStruct((ROWS, 2 * QW), f32...  122 us
    add x1, other arithmetic, local(): interpolant = noise_latents + flow_times[:, None] * velocity  2.74 us

profile of v6, /device:TPU:1, one launch (start us, length us, event | category | flops | bytes accessed | tf_op | source)
XLA Modules:
  0.0 125.9 jit_solution(7499758214025091799)
XLA Ops:
  0.6 0.0 copy-start
  0.6 0.0 copy-start.1
  0.6 122.4 %sinkhorn.1 = f32[512,512]{1,0:T(8,128)} custom-call(f32[512,512]{1,0:T(8,128)} %noise_hbm.1, f32[1024,128]{1,0:T(8,128)} %data_hbm.1), custom_call_target="tpu_custom_call" | custom-call | tf_op jit(solution)/shard_map/sinkhorn/pallas_call | solution.py:551
  123.1 0.0 copy-done
  123.1 0.0 copy-done.1
  123.1 2.7 %multiply_add_fusion = (f32[512,512]{1,0:T(8,128)}, f32[512,512]{1,0:T(8,128)}) fusion(f32[512,512]{1,0:T(8,128)S(1)} %copy-done, f32[512]{0:T(512)S(1)} %copy-done.1, f32[512,512]{1,0:T(8,128)} %sinkhorn.1), kind=kLoop, calls=%fused_computation | loop fusion | flops 786432 | bytes 4196352 | tf_op jit(solution)/shard_map/add | solution.py:573
Async XLA Ops:
  0.6 122.5 %copy-start = (f32[512,512]{1,0:T(8,128)S(1)}, f32[512,512]{1,0:T(8,128)}, u32[]{:S(2)}) copy-start(f32[512,512]{1,0:T(8,128)} %noise_hbm.1) | copy-start | bytes 3145732
  0.6 122.5 %copy-start.1 = (f32[512]{0:T(512)S(1)}, f32[512]{0:T(512)}, u32[]{:S(2)}) copy-start(f32[512]{0:T(512)} %param.5) | copy-start | bytes 6148

commit v7 on v6

--- a/solution.py
+++ b/solution.py
@@ -167,20 +167,24 @@
         return jnp.where(lax.rem(q // 2, 2) == ylo, by_shift(shift, (1, 2, jnp.where(late, 6, 5), 2)),
                          by_shift(shift, (3, jnp.where(late, 6, 5), jnp.where(late, 9, 8))))
 
+    def add_blocks(*qs):
+        for t in range(COLS // QW):
+            at, noise_at = slice(t * QW, (t + 1) * QW), slice(t * LANES, (t + 1) * LANES)
+            total, data_squares, noise_squares = scores[:, at], sq_d[at, :], sq_n[noise_at, :]
+            for q in qs:
+                total += lax.dot_general(
+                    nb[q], db[q, at, :], (((1,), (1,)), ((), ())), preferred_element_type=jnp.float32)
+                wide = db[q, at, :].astype(jnp.float32)
+                wide = wide * wide
+                data_squares = data_squares + (wide[:, :LANES] + wide[:, LANES:])
+                wide = nb[q, noise_at, :].astype(jnp.float32)
+                wide = wide * wide
+                noise_squares = noise_squares + (wide[:, :LANES] + wide[:, LANES:])
+            scores[:, at], sq_d[at, :], sq_n[noise_at, :] = total, data_squares, noise_squares
+
     def multiply(now):
         def block(q, _):
-            @pl.when(jnp.maximum(noise_level(q), data_level(q)) == now)
-            def _():
-                for t in range(COLS // QW):
-                    at, noise_at = slice(t * QW, (t + 1) * QW), slice(t * LANES, (t + 1) * LANES)
-                    scores[:, at] += lax.dot_general(
-                        nb[q], db[q, at, :], (((1,), (1,)), ((), ())), preferred_element_type=jnp.float32)
-                    wide = db[q, at, :].astype(jnp.float32)
-                    wide = wide * wide
-                    sq_d[at, :] += wide[:, :LANES] + wide[:, LANES:]
-                    wide = nb[q, noise_at, :].astype(jnp.float32)
-                    wide = wide * wide
-                    sq_n[noise_at, :] += wide[:, :LANES] + wide[:, LANES:]
+            pl.when(jnp.maximum(noise_level(q), data_level(q)) == now)(lambda: add_blocks(q))
             return 0
 
         lax.fori_loop(0, QS, block, 0)
@@ -279,7 +283,7 @@
     multiply(9)
     wait_sibling(far, 2, 0, 1)
     wait_sibling(far_mate, 2, 0, 1)
-    multiply(10)
+    add_blocks(far, far_mate)
 
     scale = LOG2E / (entropic_epsilon * D)
 
@@ -288,7 +292,7 @@
         data_row[:, at] = jnp.sum(sq_d[at, :].T, axis=0, keepdims=True)
         return 0
 
-    lax.fori_loop(0, COLS // LANES, norm_row, 0)
+    lax.fori_loop(0, COLS // LANES, norm_row, 0, unroll=4)
     group = 32
 
     def to_column(column_ref, line):

time: 126 us -> 124 us (0.984)
    pallas_call x1, Pallas kernels: 122 us -> 121 us  [local(): pl.pallas_call(kernel, out_shape=jax.ShapeDtypeStruct((ROWS, 2 * QW), f32...]
where the time goes in v7:
time: 124 us
  Pallas kernels  121 us (98%)
  other arithmetic  2.74 us (2%)
    pallas_call x1, Pallas kernels, local(): pl.pallas_call(kernel, out_shape=jax.ShapeDtypeStruct((ROWS, 2 * QW), f32...  121 us
    add x1, other arithmetic, local(): interpolant = noise_latents + flow_times[:, None] * velocity  2.74 us

profile of v7, /device:TPU:1, one launch (start us, length us, event | category | flops | bytes accessed | tf_op | source)
XLA Modules:
  0.0 124.3 jit_solution(253223443804105819)
XLA Ops:
  0.6 0.0 copy-start
  0.6 0.0 copy-start.1
  0.6 120.9 %sinkhorn.1 = f32[512,512]{1,0:T(8,128)} custom-call(f32[512,512]{1,0:T(8,128)} %noise_hbm.1, f32[1024,128]{1,0:T(8,128)} %data_hbm.1), custom_call_target="tpu_custom_call" | custom-call | tf_op jit(solution)/shard_map/sinkhorn/pallas_call | solution.py:555
  121.6 0.0 copy-done
  121.6 0.0 copy-done.1
  121.6 2.7 %multiply_add_fusion = (f32[512,512]{1,0:T(8,128)}, f32[512,512]{1,0:T(8,128)}) fusion(f32[512,512]{1,0:T(8,128)S(1)} %copy-done, f32[512]{0:T(512)S(1)} %copy-done.1, f32[512,512]{1,0:T(8,128)} %sinkhorn.1), kind=kLoop, calls=%fused_computation | loop fusion | flops 786432 | bytes 4196352 | tf_op jit(solution)/shard_map/add | solution.py:577
Async XLA Ops:
  0.6 121.0 %copy-start = (f32[512,512]{1,0:T(8,128)S(1)}, f32[512,512]{1,0:T(8,128)}, u32[]{:S(2)}) copy-start(f32[512,512]{1,0:T(8,128)} %noise_hbm.1) | copy-start | bytes 3145732
  0.6 121.0 %copy-start.1 = (f32[512]{0:T(512)S(1)}, f32[512]{0:T(512)}, u32[]{:S(2)}) copy-start(f32[512]{0:T(512)} %param.5) | copy-start | bytes 6148
